TPU v7x, 32 devices: a whole 2x2x4 slice. The times are simulated.
32 devices in a mesh: dp: 16 (over z, y, core), band: 2 (over x).
Axes of the slice: x: 2, y: 2, z: 4, core: 2. Of those that a mesh axis runs over, the one named last changes fastest.
Arguments:
- radiance: bfloat16 [16, 280, 32, 128], P('dp', 'band'), may hold values from -6 to 6
- kernel: bfloat16 [280, 7, 7], P('band'), may hold values from -0.875 to 0.875
- w_first: bfloat16 [280, 64], replicated, may hold values from -0.375 to 0.375
- w_mid: bfloat16 [64, 64], replicated, may hold values from -0.75 to 0.75
- w_out: bfloat16 [64, 280], replicated, may hold values from -0.75 to 0.75
- target: bfloat16 [16, 280, 32, 128], P('dp', None, 'band'), may hold values from -6 to 6
- mask: int32 [16, 32, 128], P('dp', 'band'), may hold values 0 or 1
Outputs:
- grad_kernel: float32 [280, 7, 7], P('band')
- grad_first: float32 [280, 64], replicated
- grad_mid: float32 [64, 64], replicated
- grad_out: float32 [64, 280], replicated
All inputs are finite; a program needn't handle non-finite values. No bound on the sum of `mask` on one device may be relied on, other than what follows from the above.
Results may differ from a plain program's by a relative error of at most 0.00056.
Values may be sent and summed in bfloat16 or wider, within the bound.
A program may use at most 64 MiB of HBM per device.

v0:
```python
import math

import jax
import jax.numpy as jnp
from jax import lax
from jax.sharding import PartitionSpec as P


def spatial(image, kernel, row_pad):
    out = lax.conv_general_dilated(
        image[None],
        kernel[:, None],
        (1, 1),
        (row_pad, (3, 3)),
        dimension_numbers=("NCHW", "OIHW", "NCHW"),
        feature_group_count=image.shape[0],
        preferred_element_type=jnp.float32,
    )
    return out[0]


def kernel_slope(image, slope, row_pad):
    out = lax.conv_general_dilated(
        image[None],
        slope[:, None],
        (1, 1),
        (row_pad, (3, 3)),
        dimension_numbers=("NCHW", "OIHW", "NCHW"),
        feature_group_count=image.shape[0],
        preferred_element_type=jnp.float32,
    )
    return out[0]


def silu_slope(value):
    sig = jax.nn.sigmoid(value)
    return sig * (1.0 + value * (1.0 - sig))


def channel_net(z_first, wanted, valid, w_mid, w_out, scale):
    hid_first = jax.nn.silu(z_first).astype(jnp.bfloat16)
    z_mid = jnp.einsum("chw,cd->dhw", hid_first, w_mid, preferred_element_type=jnp.float32)
    hid_mid = (hid_first.astype(jnp.float32) + jax.nn.silu(z_mid)).astype(jnp.bfloat16)
    predicted = jnp.einsum("chw,co->ohw", hid_mid, w_out, preferred_element_type=jnp.float32)
    err = (2.0 * scale * valid[None] * (predicted - wanted.astype(jnp.float32))).astype(
        jnp.bfloat16
    )
    grad_out = jnp.einsum("chw,ohw->co", hid_mid, err, preferred_element_type=jnp.float32)
    d_mid = jnp.einsum("co,ohw->chw", w_out, err, preferred_element_type=jnp.float32)
    dz_mid = (d_mid * silu_slope(z_mid)).astype(jnp.bfloat16)
    grad_mid = jnp.einsum("chw,dhw->cd", hid_first, dz_mid, preferred_element_type=jnp.float32)
    d_first = d_mid + jnp.einsum("cd,dhw->chw", w_mid, dz_mid, preferred_element_type=jnp.float32)
    dz_first = (d_first * silu_slope(z_first)).astype(jnp.bfloat16)
    return (dz_first, grad_mid, grad_out)


def on_device(radiance, kernel, w_first, w_mid, w_out, target, mask):
    image = radiance[0]
    wanted = target[0]
    valid = mask[0].astype(jnp.float32)
    rows_all = image.shape[1]
    scale = 1.0 / math.sqrt(lax.axis_size("dp") * rows_all * image.shape[2])
    filtered = spatial(image, kernel, (3, 3)).astype(jnp.bfloat16)
    spectra = lax.all_to_all(filtered, "band", split_axis=1, concat_axis=0, tiled=True)
    z_first = jnp.einsum("bhw,bc->chw", spectra, w_first, preferred_element_type=jnp.float32)
    dz_first, grad_mid, grad_out = channel_net(z_first, wanted, valid, w_mid, w_out, scale)
    grad_first = jnp.einsum("bhw,chw->bc", spectra, dz_first, preferred_element_type=jnp.float32)
    slope = jnp.einsum("bc,chw->bhw", w_first, dz_first, preferred_element_type=jnp.float32).astype(
        jnp.bfloat16
    )
    slope_bands = lax.all_to_all(slope, "band", split_axis=0, concat_axis=1, tiled=True)
    grad_kernel = kernel_slope(image, slope_bands, (3, 3))
    grad_first, grad_mid, grad_out = lax.psum((grad_first, grad_mid, grad_out), ("dp", "band"))
    grad_kernel = lax.psum(grad_kernel, "dp")
    return (grad_kernel, grad_first, grad_mid, grad_out)


def solution(mesh):
    in_specs = (
        P("dp", "band", None, None),
        P("band", None, None),
        P(),
        P(),
        P(),
        P("dp", None, "band", None),
        P("dp", "band", None),
    )
    out_specs = (P("band", None, None), P(), P(), P())
    return jax.shard_map(
        on_device, mesh=mesh, in_specs=in_specs, out_specs=out_specs, check_vma=False
    )
```

profile of v0, /device:TPU:0, one launch (start us, length us, event | category | flops | bytes accessed | tf_op | source)
XLA Modules:
  0.0 231.3 jit_solution(1841091035822577355)
XLA Ops:
  7.2 0.0 copy-start
  7.2 3.4 %copy.31 = bf16[1,140,32,128]{1,2,3,0:T(8,128)(2,1)S(1)} copy(bf16[1,140,32,128]{3,2,1,0:T(8,128)(2,1)} %param.7) | data formatting | bytes 2293760 | tf_op args[0]
  10.6 0.5 pad
  11.1 0.0 copy-start.7
  11.1 0.0 copy-start.8
  11.1 1.3 copy.33
  12.4 0.2 slice.2
  12.6 0.0 copy-done.7
  12.6 0.0 copy-done.8
  12.6 18.9 %select_convert_fusion = bf16[32,8,17,140]{3,1,2,0:T(8,128)(2,1)S(1)} fusion(pred[8,17]{0,1:T(8,128)(4,1)S(1)} %copy-done.8, bf16[140,32,1,7,6]{0,3,4,1,2:T(8,128)(2,1)S(1)} %slice.2, bf16[140,32,1,8,17]{0,3,4,1,2:T(8,128)(2,1)S(1)} %copy.33, bf16[140,1,7,7]{0,3,2,1:T(8,128)(2,1)S(1)} %bitcast.94), kind=kOutput, calls=%fused_computation.2 | convolution fusion | flops 62675200 | bytes 2827296 | tf_op jit(solution)/shard_map/conv_general_dilated | solution.py:10
  31.5 0.5 copy.35
  32.0 0.2 slice_bitcast_fusion
  32.2 0.0 copy-start.1
  32.2 2.8 %copy.36 = bf16[140,32,128]{2,0,1:T(8,128)(2,1)} copy(bf16[140,32,128]{0,1,2:T(8,128)(2,1)S(1)} %slice_bitcast_fusion) | data formatting | bytes 2293760 | tf_op jit(solution)/shard_map/convert_element_type | solution.py:63
  35.0 4.2 %all-to-all-start = ((bf16[140,32,128]{2,0,1:T(8,128)(2,1)}), bf16[140,32,128]{2,0,1:T(8,128)(2,1)S(1)}, u32[]{:S(2)}, u32[]{:S(2)}) async-start(bf16[140,32,128]{2,0,1:T(8,128)(2,1)} %copy.36), calls=%async_computation | async-start | bytes 2359296 | tf_op jit(solution)/shard_map/all_to_all | solution.py:64
  39.2 0.0 copy-done.1
  39.2 0.0 copy-start.5
  39.3 5.1 %copy.44 = bf16[1,140,32,128]{1,0,3,2:T(2,128)(2,1)} copy(bf16[1,140,32,128]{3,2,1,0:T(8,128)(2,1)S(1)} %copy-done.1) | data formatting | bytes 2293760 | tf_op args[0]
  44.3 0.0 copy-done.5
  44.4 0.0 copy-start.3
  44.4 10.7 %all-to-all-done = bf16[140,32,128]{2,0,1:T(8,128)(2,1)S(1)} async-done(((bf16[140,32,128]{2,0,1:T(8,128)(2,1)}), bf16[140,32,128]{2,0,1:T(8,128)(2,1)S(1)}, u32[]{:S(2)}, u32[]{:S(2)}) %all-to-all-start) | async-done | bytes 1146912 | tf_op jit(solution)/shard_map/all_to_all | solution.py:64
  55.1 0.3 copy.38
  55.4 0.0 copy-start.4
  55.4 0.0 copy-done.3
  55.4 0.0 copy-start.6
  55.4 0.4 multiply_convert_fusion.1
  55.9 0.2 copy-done.4
  56.1 0.3 convolution_bitcast_fusion.2
  56.4 0.0 copy-done
  56.4 0.3 copy-done.6
  56.7 0.6 fusion.9
  57.3 0.0 copy-start.9
  57.3 0.5 multiply_convert_fusion
  57.8 0.6 copy-done.9
  58.3 0.3 fusion.16
  58.6 0.0 copy-start.2
  58.6 0.5 fusion.13
  59.1 1.2 copy.42
  60.3 0.0 copy-done.2
  60.3 3.6 %all-to-all-start.1 = ((bf16[280,16,128]{2,1,0:T(8,128)(2,1)}), bf16[280,16,128]{2,1,0:T(8,128)(2,1)S(1)}, u32[]{:S(2)}, u32[]{:S(2)}) async-start(bf16[280,16,128]{2,1,0:T(8,128)(2,1)} %copy.42), calls=%async_computation.1 | async-start | bytes 2293760 | tf_op jit(solution)/shard_map/all_to_all | solution.py:71
  63.9 0.0 all-reduce.3.cloned.1.call-start
  63.9 2.1 convolution_bitcast_fusion.5
  66.0 2.4 %convolution_bitcast_fusion.4 = f32[64,280]{1,0:T(8,128)} fusion(bf16[280,16,128]{2,0,1:T(8,128)(2,1)} %copy-done.9, f32[64,16,128]{2,0,1:T(8,128)S(1)} %convolution_bitcast_fusion.2, bf16[64,16,128]{2,0,1:T(8,128)(2,1)S(1)} %get-tuple-element.6), kind=kOutput, calls=%fused_computation.23 | convolution fusion | flops 74317824 | bytes 2004992 | tf_op jit(solution)/shard_map/chw,ohw->co/dot_general | solution.py:48
  68.4 0.0 all-reduce.3.cloned.1.call-update
  68.5 0.2 convolution_bitcast_fusion.6
  68.7 44.7 %psum.30 = f32[64,64]{1,0:T(8,128)} all-reduce(f32[64,64]{1,0:T(8,128)S(1)} %convolution_bitcast_fusion.6), channel_id=1, replica_groups=mesh['dp'=16,'band'=2] {'dp','band'}, use_global_device_ids=true, to_apply=%region_2.3 | all-reduce | flops 4096 | bytes 32768 | tf_op jit(solution)/shard_map/psum | solution.py:73
  113.3 0.0 all-to-all-done.1
  113.3 0.2 copy.43
  113.5 5.2 %copy.45 = bf16[140,1,32,128]{0,1,3,2:T(2,128)(2,1)} copy(bf16[140,1,32,128]{3,2,0,1:T(8,128)(2,1)S(1)} %bitcast.90) | data formatting | bytes 2293760 | tf_op jit(solution)/shard_map/broadcast_in_dim | solution.py:25
  118.7 43.5 %fusion.29 = f32[1,140,7,7]{1,0,3,2:T(1,128)S(1)} fusion(bf16[1,140,32,128]{1,0,3,2:T(2,128)(2,1)} %copy.44, bf16[140,1,32,128]{0,1,3,2:T(2,128)(2,1)} %copy.45), kind=kOutput, calls=%fused_computation.45 | convolution fusion | flops 52474240 | bytes 2321200 | tf_op jit(solution)/shard_map/conv_general_dilated | solution.py:23
  162.2 59.2 %psum.28 = f32[140,7,7]{0,2,1:T(8,128)} all-reduce(f32[140,7,7]{0,2,1:T(8,128)S(1)} %bitcast.93), channel_id=1, replica_groups=mesh['dp'=16,'band'=2] {'dp'}, use_global_device_ids=true, to_apply=%region_0.1 | all-reduce | flops 6860 | bytes 54880 | tf_op jit(solution)/shard_map/psum | solution.py:74
  221.4 0.0 all-reduce.3.cloned.1.call-done
  221.4 1.5 copy.65
  222.9 1.5 copy.66
  (2 shorter events, 0.0 us)
Async XLA Ops:
  7.2 49.2 %copy-start = (bf16[64,280]{1,0:T(8,128)(2,1)S(1)}, bf16[64,280]{1,0:T(8,128)(2,1)}, u32[]{:S(2)}) copy-start(bf16[64,280]{1,0:T(8,128)(2,1)} %param.11) | copy-start | bytes 107524
  11.1 1.5 copy-start.7
  11.1 1.5 copy-start.8
  32.2 7.0 %copy-start.1 = (bf16[1,140,32,128]{3,2,1,0:T(8,128)(2,1)S(1)}, bf16[1,140,32,128]{3,2,1,0:T(8,128)(2,1)}, u32[]{:S(2)}) copy-start(bf16[1,140,32,128]{3,2,1,0:T(8,128)(2,1)} %param.7) | copy-start | bytes 3440644
  35.0 20.1 %all-to-all-start = ((bf16[140,32,128]{2,0,1:T(8,128)(2,1)}), bf16[140,32,128]{2,0,1:T(8,128)(2,1)S(1)}, u32[]{:S(2)}, u32[]{:S(2)}) async-start(bf16[140,32,128]{2,0,1:T(8,128)(2,1)} %copy.36), calls=%async_computation | async-start | bytes 2359296 | tf_op jit(solution)/shard_map/all_to_all | solution.py:64
  39.2 5.1 %copy-start.5 = (s32[1,16,128]{2,1,0:T(8,128)S(1)}, s32[1,16,128]{2,1,0:T(8,128)}, u32[]{:S(2)}) copy-start(s32[1,16,128]{2,1,0:T(8,128)} %param.13) | copy-start | bytes 24580
  44.4 11.1 %copy-start.3 = (bf16[280,64]{0,1:T(8,128)(2,1)S(1)}, bf16[280,64]{0,1:T(8,128)(2,1)}, u32[]{:S(2)}) copy-start(bf16[280,64]{0,1:T(8,128)(2,1)} %param.9) | copy-start | bytes 107524
  55.4 0.7 copy-start.4
  55.4 1.3 copy-start.6
  57.3 1.0 copy-start.9
  58.6 1.7 copy-start.2
  60.3 53.0 %all-to-all-start.1 = ((bf16[280,16,128]{2,1,0:T(8,128)(2,1)}), bf16[280,16,128]{2,1,0:T(8,128)(2,1)S(1)}, u32[]{:S(2)}, u32[]{:S(2)}) async-start(bf16[280,16,128]{2,1,0:T(8,128)(2,1)} %copy.42), calls=%async_computation.1 | async-start | bytes 2293760 | tf_op jit(solution)/shard_map/all_to_all | solution.py:71
  63.9 157.5 %all-reduce.3.cloned.1.call-start = ((), (), s32[]{:S(2)}) async-start(), calls=%async_computation.2 | async-start | bytes 393216 | tf_op jit(solution)/shard_map/psum | solution.py:73
Sparse Core Ops, SparseCore 0:
  70.9 125.5 all-reduce.2
where the time goes:
time: 232 us; the launch traced here: 231 us
  blocking collectives  104 us (45%)
  matrix products  69.6 us (30%)
  local copies, waits for them, and re-layouts  25 us (11%)
  between operations  14.3 us (6%)
  waiting for transfers between devices  10.8 us (5%)
  starting transfers between devices  7.84 us (3%)
    psum x1, blocking collectives, on_device(): grad_kernel = lax.psum(grad_kernel, 'dp')  59.2 us
    psum x1, blocking collectives, on_device(): lax.psum((grad_first, grad_mid, grad_out), ('dp', 'band'))  44.7 us
    conv_general_dilated x1, matrix products, kernel_slope(): lax.conv_general_dilated(image[None], slope[:, None], (1, 1), (row_pad, (...  43.5 us
    conv_general_dilated x1, matrix products, spatial(): lax.conv_general_dilated(image[None], kernel[:, None], (1, 1), (row_pad,...  18.9 us
    unnamed x26, local copies, waits for them, and re-layouts  13.2 us
    all_to_all x1, waiting for transfers between devices, on_device(): lax.all_to_all(filtered, 'band', split_axis=1, concat_axis=0, tiled=True)  10.7 us
    broadcast_in_dim x1, local copies, waits for them, and re-layouts, kernel_slope(): slope[:, None]  5.16 us
  transfers between devices with their start and end apart: 3, of which 1 were waited for; matrix products, arithmetic and copies ran while one was open for 25% of the time, Pallas kernels for 0%

commit v1 on v0

v1 whole, which is shorter than its diff:
```python
import functools
import math

import jax
import jax.numpy as jnp
from jax import lax
from jax.experimental import pallas as pl
from jax.experimental.pallas import tpu as pltpu
from jax.sharding import PartitionSpec as P

MESH = pl.DeviceIdType.MESH
F32 = jnp.float32
BF16 = jnp.bfloat16
PACK = 4


def up(value, step):
    return -(-value // step) * step


def mm(a, b):
    return jnp.dot(a, b, preferred_element_type=F32)


def mm_nt(a, b):
    return lax.dot_general(a, b, (((1,), (1,)), ((), ())), preferred_element_type=F32)


def kernel(
    cfg,
    x_ref, taps_ref, wft_ref, wf_ref, wm_ref, wmt_ref, wo_ref, wot_ref, target_ref, mask_ref,
    gk_ref, gf_ref, gm_ref, go_ref,
    stack, filt, slope, z_send, z_recv, dz_all, hid_s,
    early, early_in, early_out, late, late_in,
    z_ss, z_rs, d_ss, d_rs, e_ss, e_rs, ea_ss, ea_rs, l_ss, l_rs, la_ss, la_rs,
):
    nd, nb = cfg["nd"], cfg["nb"]
    bands, groups, bp, ks = cfg["bands"], cfg["groups"], cfg["bp"], cfg["ks"]
    rows_all, rows, width, chunks = cfg["rows_all"], cfg["rows"], cfg["width"], cfg["chunks"]
    ch, outs, scale = cfg["ch"], cfg["outs"], cfg["scale"]
    ew, lw = cfg["ew"], cfg["lw"]
    half = ks // 2
    lanes = 8 * rows_all
    step_rows = rows // chunks
    me_d = lax.axis_index("dp")
    me_b = lax.axis_index("band")
    me = me_d * nb + me_b
    total = nd * nb

    def device(index):
        return (index // nb, lax.rem(index, nb))

    barrier = pltpu.get_barrier_semaphore()

    def greet(k, _):
        pl.semaphore_signal(
            barrier, inc=1, device_id=device(lax.rem(me + k, total)), device_id_type=MESH
        )
        return 0

    lax.fori_loop(1, total, greet, 0)

    row_i = lax.broadcasted_iota(jnp.int32, (rows_all, lanes), 0)
    lane_i = lax.broadcasted_iota(jnp.int32, (rows_all, lanes), 1)
    block = lane_i // rows_all
    tap = lane_i % rows_all - row_i + half
    band_mask = (tap >= 0) & (tap < ks) & (block < ks)
    col = lax.broadcasted_iota(jnp.int32, (rows_all, width), 1)
    tail = bp - 16
    for h in range(rows_all):
        filt[pl.ds(h * bp + tail, 16), :] = jnp.zeros((16, width), F32)

    def filter_group(g, _):
        packed = pltpu.roll(taps_ref[pl.ds(g, 1), :], 8 - half, 1)
        spread = jnp.broadcast_to(packed, (rows_all, lanes))
        for q in range(PACK):
            b = jnp.minimum(g * PACK + q, bands - 1)
            image = x_ref[b].astype(F32)
            parts = []
            for j in range(ks):
                s = j - half
                if s == 0:
                    moved = image
                else:
                    moved = pltpu.roll(image, (-s) % width, 1)
                    moved = jnp.where((col + s >= 0) & (col + s < width), moved, 0.0)
                parts.append(moved.astype(BF16))
            parts.append(jnp.zeros((lanes - ks * rows_all, width), BF16))
            moved_all = jnp.concatenate(parts, axis=0)
            stack[g * PACK + q] = moved_all
            taps = pltpu.roll(
                spread, lanes - 8 - 8 * q, 1, stride=1, stride_axis=0
            )
            taps = jnp.where(band_mask, taps, 0.0).astype(BF16)
            out = mm(taps, moved_all)
            filt[pl.ds(g * PACK + q, rows_all, stride=bp), :] = out.astype(BF16).astype(F32)
        return 0

    lax.fori_loop(0, groups, filter_group, 0)

    def filt_rows(h, count):
        return jnp.concatenate(
            [
                filt[pl.ds(pl.multiple_of((h + r) * bp, 8), bp), :].astype(BF16)
                for r in range(count)
            ],
            axis=1,
        )

    pl.semaphore_wait(barrier, total - 1)

    def z_copy(k, c):
        part = pl.ds(c * step_rows, step_rows)
        return pltpu.make_async_remote_copy(
            src_ref=z_send.at[k, part],
            dst_ref=z_recv.at[k, part],
            send_sem=z_ss.at[k, c],
            recv_sem=z_rs.at[k, c],
            device_id=(me_d, lax.rem(me_b + k, nb)),
            device_id_type=MESH,
        )

    def z_part(k, c):
        owner = lax.rem(me_b + k, nb)

        def one(p, _):
            h = c * step_rows + p * 2
            z = mm(wft_ref[...], filt_rows(owner * rows + h, 2))
            z_send[k, h] = z[:, :width]
            z_send[k, h + 1] = z[:, width:]
            return 0

        lax.fori_loop(0, step_rows // 2, one, 0, unroll=True)

    for k in range(1, nb):
        for c in range(chunks):
            z_part(k, c)
            z_copy(k, c).start()
    for c in range(chunks):
        z_part(0, c)

    def d_copy(k, c):
        part = pl.ds(me_b * rows + c * step_rows, step_rows)
        return pltpu.make_async_remote_copy(
            src_ref=dz_all.at[part],
            dst_ref=dz_all.at[part],
            send_sem=d_ss.at[k, c],
            recv_sem=d_rs.at[k, c],
            device_id=(me_d, lax.rem(me_b + k, nb)),
            device_id_type=MESH,
        )

    def wide(pieces):
        return jnp.concatenate(pieces, axis=1)

    g_out = jnp.zeros((ch, outs), F32)
    g_mid = jnp.zeros((ch, ch), F32)
    for c in range(chunks):
        for k in range(1, nb):
            z_copy(k, c).wait_recv()
        z_list = []
        for r in range(step_rows):
            h = c * step_rows + r
            z = z_send[0, h]
            for k in range(1, nb):
                z = z + z_recv[k, h]
            z_list.append(z)
        z_first = wide(z_list)
        sig_first = jax.nn.sigmoid(z_first)
        hid_first = (z_first * sig_first).astype(BF16)
        z_mid = mm(wmt_ref[...], hid_first)
        sig_mid = jax.nn.sigmoid(z_mid)
        hid_mid = (hid_first.astype(F32) + z_mid * sig_mid).astype(BF16)
        predicted = mm(wot_ref[...], hid_mid)
        errs = []
        for r in range(step_rows):
            h = c * step_rows + r
            factor = (2.0 * scale) * mask_ref[pl.ds(h, 1), :].astype(F32)
            diff = predicted[:, r * width:(r + 1) * width] - target_ref[h].astype(F32)
            errs.append((factor * diff).astype(BF16))
        err = wide(errs)
        g_out = g_out + mm_nt(hid_mid, err)
        d_mid = mm(wo_ref[...], err)
        dz_mid = (d_mid * (sig_mid * (1.0 + z_mid * (1.0 - sig_mid)))).astype(BF16)
        g_mid = g_mid + mm_nt(hid_first, dz_mid)
        d_first = d_mid + mm(wm_ref[...], dz_mid)
        dz = (d_first * (sig_first * (1.0 + z_first * (1.0 - sig_first)))).astype(BF16)
        for r in range(step_rows):
            h = c * step_rows + r
            dz_all[me_b * rows + h] = dz[:, r * width:(r + 1) * width]
        for k in range(1, nb):
            d_copy(k, c).start()

    hid_s[...] = jnp.zeros_like(hid_s)

    def slope_rows(first):
        def one(p, _):
            h = first + 2 * p
            dz = wide([dz_all[h], dz_all[h + 1]])
            hid_s[...] += mm_nt(dz, filt_rows(h, 2))
            back = mm(wf_ref[...], dz)
            for r in range(2):
                place = pl.multiple_of((rows_all - 1 - h - r) * bp, 8)
                slope[pl.ds(place, bp), :] = back[:, r * width:(r + 1) * width]
            return 0

        lax.fori_loop(0, step_rows // 2, one, 0, unroll=True)

    for c in range(chunks):
        slope_rows(me_b * rows + c * step_rows)
    for k in range(1, nb):
        source = lax.rem(me_b + nb - k, nb)
        for c in range(chunks):
            d_copy(k, c).wait_recv()
            slope_rows(source * rows + c * step_rows)

    def piece(ref, index, w):
        lane_parts = nd // 8
        each = w // lane_parts
        return ref.at[
            pl.ds(pl.multiple_of((index // lane_parts) * 8, 8), 8),
            pl.ds(pl.multiple_of(lax.rem(index, lane_parts) * each, 128), each),
        ]

    def scatter_copy(ref, into, w, ss, rs, k):
        peer = lax.rem(me_d + k, nd)
        return pltpu.make_async_remote_copy(
            src_ref=piece(ref, peer, w),
            dst_ref=into.at[k],
            send_sem=ss.at[k],
            recv_sem=rs.at[k],
            device_id=(peer, me_b),
            device_id_type=MESH,
        )

    def each(count, act):
        def body(k, _):
            act(k)
            return 0

        lax.fori_loop(1, count, body, 0)

    def gather_early(k):
        part = piece(early_out.at[me_b], me_d, ew)
        return pltpu.make_async_remote_copy(
            src_ref=part,
            dst_ref=part,
            send_sem=ea_ss.at[k],
            recv_sem=ea_rs.at[k],
            device_id=device(lax.rem(me + k, total)),
            device_id_type=MESH,
        )

    def gather_late(k):
        part = piece(gk_ref, me_d, lw)
        return pltpu.make_async_remote_copy(
            src_ref=part,
            dst_ref=part,
            send_sem=la_ss.at[k],
            recv_sem=la_rs.at[k],
            device_id=(lax.rem(me_d + k, nd), me_b),
            device_id_type=MESH,
        )

    early[...] = jnp.zeros_like(early)
    early[:, 0:outs] = g_out
    early[:, outs:outs + ch] = g_mid
    early[:, outs + ch:outs + ch + bands] = hid_s[:, 0:bands]
    each(nd, lambda k: scatter_copy(early, early_in, ew, e_ss, e_rs, k).start())
    late[...] = jnp.zeros_like(late)

    h_i = rows_all - 1 - row_i
    skew = lanes - (rows_all - 1) + half
    extra = -skew % 8
    lane_e = jnp.maximum(lane_i - extra, 0)
    block_e = jnp.where(lane_i >= extra, lane_e // rows_all, ks)
    tap_e = lane_e % rows_all

    def taps_group(g, _):
        acc = jnp.zeros((rows_all, lanes), F32)
        for q in range(PACK):
            b = g * PACK + q
            rows_b = slope[pl.ds(b, rows_all, stride=bp), :].astype(BF16)
            cross = mm_nt(rows_b, stack[b])
            place = 8 * q
            moved = pltpu.roll(
                cross, (skew + extra + place) % lanes, 1, stride=1, stride_axis=0
            )
            i = tap_e - place
            source = h_i + i - half
            valid = (i >= 0) & (i < ks) & (source >= 0) & (source < rows_all) & (block_e < ks)
            acc = acc + jnp.where(valid, moved, 0.0)
        summed = jnp.sum(acc, axis=0, keepdims=True)
        late[pl.ds(g, 1), 0:lanes] = pltpu.roll(summed, lanes - extra, 1)
        return 0

    cut = groups // 2
    lax.fori_loop(0, cut, taps_group, 0)

    each(nd, lambda k: scatter_copy(early, early_in, ew, e_ss, e_rs, k).wait_recv())
    own = piece(early, me_d, ew)[...]
    for k in range(1, nd):
        own = own + early_in[k]
    piece(early_out.at[me_b], me_d, ew)[...] = own
    each(total, lambda k: gather_early(k).start())

    lax.fori_loop(cut, groups, taps_group, 0)

    each(nd, lambda k: scatter_copy(late, late_in, lw, l_ss, l_rs, k).start())
    each(total, lambda k: gather_early(k).wait_recv())
    result = early_out[0]
    for k in range(1, nb):
        result = result + early_out[k]
    go_ref[...] = result[:, 0:outs]
    gm_ref[...] = result[:, outs:outs + ch]
    for k in range(nb):
        gf_ref[:, k * bands:(k + 1) * bands] = early_out[k, :, outs + ch:outs + ch + bands]

    each(nd, lambda k: scatter_copy(late, late_in, lw, l_ss, l_rs, k).wait_recv())
    own = piece(late, me_d, lw)[...]
    for k in range(1, nd):
        own = own + late_in[k]
    piece(gk_ref, me_d, lw)[...] = own
    each(nd, lambda k: gather_late(k).start())
    each(nd, lambda k: gather_late(k).wait_recv())

    for k in range(1, nb):
        for c in range(chunks):
            z_copy(k, c).wait_send()
            d_copy(k, c).wait_send()
    each(nd, lambda k: scatter_copy(early, early_in, ew, e_ss, e_rs, k).wait_send())
    each(total, lambda k: gather_early(k).wait_send())
    each(nd, lambda k: scatter_copy(late, late_in, lw, l_ss, l_rs, k).wait_send())
    each(nd, lambda k: gather_late(k).wait_send())


def on_device(nd, nb, radiance, kernel_taps, w_first, w_mid, w_out, target, mask):
    image = radiance[0]
    bands, rows_all, width = image.shape
    ks = kernel_taps.shape[1]
    ch = w_first.shape[1]
    outs = w_out.shape[1]
    rows = rows_all // nb
    chunks = 2
    groups = -(-bands // PACK)
    bp = up(groups * PACK, 16)
    lane_parts = nd // 8
    ew = up(outs + ch + bands, 128 * lane_parts)
    lw = up(8 * rows_all, 128 * lane_parts)
    cfg = dict(
        nd=nd, nb=nb, bands=bands, groups=groups, bp=bp, ks=ks, rows_all=rows_all, rows=rows,
        width=width, chunks=chunks, ch=ch, outs=outs, ew=ew, lw=lw,
        scale=1.0 / math.sqrt(nd * rows_all * width),
    )
    taps = jnp.pad(kernel_taps, ((0, groups * PACK - bands), (0, 8 - ks), (0, 8 - ks)))
    taps = taps.reshape(groups, PACK, 8, 8).transpose(0, 3, 1, 2).reshape(groups, 8 * PACK * 8)
    own = lax.dynamic_slice_in_dim(w_first, lax.axis_index("band") * bands, bands, 0)
    own = jnp.pad(own, ((0, bp - bands), (0, 0)))
    sems = lambda *shape: pltpu.SemaphoreType.DMA(shape)
    lanes = 8 * rows_all
    packed, g_first, g_mid, g_out = pl.pallas_call(
        functools.partial(kernel, cfg),
        out_shape=(
            jax.ShapeDtypeStruct((64, lw), F32),
            jax.ShapeDtypeStruct((ch, bands * nb), F32),
            jax.ShapeDtypeStruct((ch, ch), F32),
            jax.ShapeDtypeStruct((ch, outs), F32),
        ),
        in_specs=[pl.BlockSpec(memory_space=pltpu.VMEM)] * 10,
        out_specs=(pl.BlockSpec(memory_space=pltpu.VMEM),) * 4,
        scratch_shapes=[
            pltpu.VMEM((groups * PACK, lanes, width), BF16),
            pltpu.VMEM((rows_all * bp, width), F32),
            pltpu.VMEM((rows_all * bp, width), F32),
            pltpu.VMEM((nb, rows, ch, width), F32),
            pltpu.VMEM((nb, rows, ch, width), F32),
            pltpu.VMEM((rows_all, ch, width), BF16),
            pltpu.VMEM((ch, bp), F32),
            pltpu.VMEM((64, ew), F32),
            pltpu.VMEM((nd, 8, ew // lane_parts), F32),
            pltpu.VMEM((nb, 64, ew), F32),
            pltpu.VMEM((64, lw), F32),
            pltpu.VMEM((nd, 8, lw // lane_parts), F32),
            sems(nb, chunks), sems(nb, chunks), sems(nb, chunks), sems(nb, chunks),
            sems(nd), sems(nd), sems(nd * nb), sems(nd * nb),
            sems(nd), sems(nd), sems(nd), sems(nd),
        ],
        compiler_params=pltpu.CompilerParams(
            collective_id=0, has_side_effects=True, vmem_limit_bytes=56 * 1024 * 1024
        ),
    )(
        image, taps.astype(F32), own.T, own, w_mid, w_mid.T, w_out, w_out.T,
        target[0].transpose(1, 0, 2), mask[0],
    )
    g_taps = packed[:groups, :lanes].reshape(groups, 8, PACK, 8).transpose(0, 2, 3, 1)
    g_taps = g_taps.reshape(groups * PACK, 8, 8)[:bands, :ks, :ks]
    return (g_taps, g_first.T, g_mid, g_out)


def solution(mesh):
    in_specs = (
        P("dp", "band", None, None),
        P("band", None, None),
        P(),
        P(),
        P(),
        P("dp", None, "band", None),
        P("dp", "band", None),
    )
    out_specs = (P("band", None, None), P(), P(), P())
    return jax.shard_map(
        functools.partial(on_device, mesh.shape["dp"], mesh.shape["band"]),
        mesh=mesh, in_specs=in_specs, out_specs=out_specs, check_vma=False,
    )
```

time: 232 us -> 73.3 us (0.32)
  blocking collectives: 104 us -> 0 us
  matrix products: 69.6 us -> 0 us
  Pallas kernels: 0 us -> 59.7 us
  between operations: 14.3 us -> 0.71 us
  local copies, waits for them, and re-layouts: 25 us -> 11.8 us
  waiting for transfers between devices: 10.8 us -> 0 us
  starting transfers between devices: 7.84 us -> 0 us
    psum x2 -> x0, blocking collectives: 104 us -> none  [the longest x1 59.2 us: on_device(): grad_kernel = lax.psum(grad_kernel, 'dp')]
    conv_general_dilated x2 -> x0, matrix products: 62.3 us -> none  [the longest x1 43.5 us: kernel_slope(): lax.conv_general_dilated(image[None], slope[:, None], (1, 1), (row_pad, (...]
    pallas_call x0 -> x1, Pallas kernels: none -> 59.7 us  [on_device(): pl.pallas_call(functools.partial(kernel, cfg), out_shape=(jax.ShapeDtypeS...]
    all_to_all x2 -> x0, waiting for transfers between devices: 10.8 us -> none  [the longest x1 10.7 us: on_device(): lax.all_to_all(filtered, 'band', split_axis=1, concat_axis=0, tiled=True)]
    all_to_all x2 -> x0, starting transfers between devices: 7.8 us -> none  [the longest x1 4.21 us: on_device(): lax.all_to_all(filtered, 'band', split_axis=1, concat_axis=0, tiled=True)]
    dot_general x9 -> x0, matrix products: 7.24 us -> none  [the longest x1 2.39 us: channel_net(): jnp.einsum('chw,ohw->co', hid_mid, err, preferred_element_type=jnp.float32)]
    unnamed x26 -> x18, local copies, waits for them, and re-layouts: 13.2 us -> 7.32 us
    broadcast_in_dim x1 -> x0, local copies, waits for them, and re-layouts: 5.16 us -> none  [kernel_slope(): slope[:, None]]
  transfers between devices with their start and end apart: 3 -> 0, of which waited for: 1 -> 0; matrix products, arithmetic and copies ran while one was open for 25% -> 0% of each run, Pallas kernels for 0% -> 0%
where the time goes in v1:
time: 73.3 us; the launch traced here: 73 us
  Pallas kernels  59.7 us (81%)
  local copies, waits for them, and re-layouts  11.8 us (16%)
  other arithmetic  0.75 us (1%)
    pallas_call x1, Pallas kernels, on_device(): pl.pallas_call(functools.partial(kernel, cfg), out_shape=(jax.ShapeDtypeS...  59.7 us
    unnamed x18, local copies, waits for them, and re-layouts  7.32 us
    convert_element_type x3, local copies, waits for them, and re-layouts, on_device(): taps.astype(F32)  1.54 us

profile of v1, /device:TPU:0, one launch (start us, length us, event | category | flops | bytes accessed | tf_op | source)
XLA Modules:
  0.0 73.0 jit_solution(10988098014895140613)
XLA Ops:
  0.6 0.0 copy-start
  0.6 0.0 copy-start.1
  0.7 1.5 %copy.21 = bf16[64,64]{0,1:T(8,128)(2,1)} copy(bf16[64,64]{1,0:T(8,128)(2,1)} %wm_ref.1) | data formatting | bytes 16384 | tf_op args[3]
  2.2 0.0 copy-done
  2.2 0.1 constant_dynamic-slice_fusion
  2.2 0.1 copy.29
  2.4 0.6 fusion
  3.0 0.7 copy.25.wft_ref
  3.7 0.8 %pad_convert_fusion = f32[140,8,8]{0,2,1:T(8,128)S(1)} fusion(bf16[140,7,7]{0,2,1:T(8,128)(2,1)} %param.8), kind=kLoop, calls=%fused_computation.1 | loop fusion | flops 8960 | bytes 49560 | tf_op jit(solution)/shard_map/convert_element_type | solution.py:392
  4.5 1.5 %copy.22 = bf16[64,280]{0,1:T(8,128)(2,1)} copy(bf16[64,280]{1,0:T(8,128)(2,1)} %wo_ref.1) | data formatting | bytes 71680 | tf_op args[4]
  6.0 0.4 copy.18
  6.4 0.5 copy.19
  6.8 0.7 copy.24.taps_ref
  7.5 0.0 copy-done.1
  7.6 1.3 %copy.31 = bf16[1,280,16,128]{3,1,2,0:T(8,128)(2,1)} copy(bf16[1,280,16,128]{3,2,1,0:T(8,128)(2,1)S(1)} %copy-done.1) | data formatting | bytes 2293760 | tf_op args[5]
  8.9 59.7 %shard_map.102 = (f32[64,256]{1,0:T(8,128)}, f32[64,280]{1,0:T(8,128)}, f32[64,64]{1,0:T(8,128)}, f32[64,280]{1,0:T(8,128)}) custom-call(bf16[140,32,128]{2,1,0:T(8,128)(2,1)} %bitcast.24, f32[35,256]{1,0:T(8,128)} %copy.24.taps_ref, bf16[64,144]{1,0:T(8,128)(2,1)} %copy.25.wft_ref, bf16[144,64]{1,0:T(8,128)(2,1)} %get-tuple-element.16.wf_ref, ...), custom_call_target="tpu_custom_call" | custom-call | tf_op jit(solution)/shard_map/pallas_call | solution.py:361
  68.6 0.0 copy-start.3
  68.6 0.0 copy-start.4
  68.6 0.0 copy-start.2
  68.6 0.8 %slice.6 = f32[35,256]{1,0:T(8,128)S(1)} slice(f32[64,256]{1,0:T(8,128)} %get-tuple-element.8), slice={[0:35], [0:256]} | slice | bytes 71680 | tf_op jit(solution)/shard_map/slice | solution.py:395
  69.4 0.1 copy.26
  69.5 0.6 copy.27
  70.1 1.0 %copy.28 = f32[140,7,7]{0,2,1:T(8,128)} copy(f32[140,7,7]{2,1,0:T(8,128)S(1)} %bitcast.23) | data formatting | bytes 54880
  71.1 0.0 copy-done.3
  71.1 0.6 copy.35
  71.7 0.0 copy-done.4
  71.7 0.6 copy.36
  72.3 0.0 copy-done.2
  72.3 0.6 copy.37
Async XLA Ops:
  0.6 1.5 %copy-start = (bf16[280,64]{0,1:T(8,128)(2,1)S(1)}, bf16[280,64]{0,1:T(8,128)(2,1)}, u32[]{:S(2)}) copy-start(bf16[280,64]{0,1:T(8,128)(2,1)} %param.9) | copy-start | bytes 107524
  0.6 6.9 %copy-start.1 = (bf16[1,280,16,128]{3,2,1,0:T(8,128)(2,1)S(1)}, bf16[1,280,16,128]{3,2,1,0:T(8,128)(2,1)}, u32[]{:S(2)}) copy-start(bf16[1,280,16,128]{3,2,1,0:T(8,128)(2,1)} %param.12) | copy-start | bytes 3440644
  68.6 2.5 %copy-start.3 = (f32[64,280]{1,0:T(8,128)S(1)}, f32[64,280]{1,0:T(8,128)}, u32[]{:S(2)}) copy-start(f32[64,280]{1,0:T(8,128)} %get-tuple-element.9) | copy-start | bytes 215044
  68.6 3.1 %copy-start.4 = (f32[64,64]{1,0:T(8,128)S(1)}, f32[64,64]{1,0:T(8,128)}, u32[]{:S(2)}) copy-start(f32[64,64]{1,0:T(8,128)} %get-tuple-element.24) | copy-start | bytes 49156
  68.6 3.7 %copy-start.2 = (f32[64,280]{1,0:T(8,128)S(1)}, f32[64,280]{1,0:T(8,128)}, u32[]{:S(2)}) copy-start(f32[64,280]{1,0:T(8,128)} %get-tuple-element.25) | copy-start | bytes 215044

commit v2 on v1

--- a/solution.py
+++ b/solution.py
@@ -11,7 +11,6 @@
 MESH = pl.DeviceIdType.MESH
 F32 = jnp.float32
 BF16 = jnp.bfloat16
-PACK = 4
 
 
 def up(value, step):
@@ -22,20 +21,29 @@
     return jnp.dot(a, b, preferred_element_type=F32)
 
 
+def mm_tn(a, b):
+    return lax.dot_general(a, b, (((0,), (0,)), ((), ())), preferred_element_type=F32)
+
+
+def eye(n):
+    same = lax.broadcasted_iota(jnp.int32, (n, n), 0) == lax.broadcasted_iota(jnp.int32, (n, n), 1)
+    return jnp.where(same, 1.0, 0.0).astype(BF16)
+
+
 def mm_nt(a, b):
     return lax.dot_general(a, b, (((1,), (1,)), ((), ())), preferred_element_type=F32)
 
 
 def kernel(
     cfg,
-    x_ref, taps_ref, wft_ref, wf_ref, wm_ref, wmt_ref, wo_ref, wot_ref, target_ref, mask_ref,
+    x_ref, taps_ref, w1t_ref, wm_ref, wo_ref, target_ref, mask_ref,
     gk_ref, gf_ref, gm_ref, go_ref,
-    stack, filt, slope, z_send, z_recv, dz_all, hid_s,
+    tap_rows, taps_own, wft_ref, wf_ref, wmt_ref, wot_ref, wanted, sums, stack, filt, slope, z_send, z_recv, dz_all, hid_s,
     early, early_in, early_out, late, late_in,
     z_ss, z_rs, d_ss, d_rs, e_ss, e_rs, ea_ss, ea_rs, l_ss, l_rs, la_ss, la_rs,
 ):
     nd, nb = cfg["nd"], cfg["nb"]
-    bands, groups, bp, ks = cfg["bands"], cfg["groups"], cfg["bp"], cfg["ks"]
+    bands, unroll, bp, ks = cfg["bands"], cfg["unroll"], cfg["bp"], cfg["ks"]
     rows_all, rows, width, chunks = cfg["rows_all"], cfg["rows"], cfg["width"], cfg["chunks"]
     ch, outs, scale = cfg["ch"], cfg["outs"], cfg["scale"]
     ew, lw = cfg["ew"], cfg["lw"]
@@ -46,6 +54,7 @@
     me_b = lax.axis_index("band")
     me = me_d * nb + me_b
     total = nd * nb
+    split = nb == 2
 
     def device(index):
         return (index // nb, lax.rem(index, nb))
@@ -66,37 +75,68 @@
     tap = lane_i % rows_all - row_i + half
     band_mask = (tap >= 0) & (tap < ks) & (block < ks)
     col = lax.broadcasted_iota(jnp.int32, (rows_all, width), 1)
-    tail = bp - 16
     for h in range(rows_all):
-        filt[pl.ds(h * bp + tail, 16), :] = jnp.zeros((16, width), F32)
-
-    def filter_group(g, _):
-        packed = pltpu.roll(taps_ref[pl.ds(g, 1), :], 8 - half, 1)
-        spread = jnp.broadcast_to(packed, (rows_all, lanes))
-        for q in range(PACK):
-            b = jnp.minimum(g * PACK + q, bands - 1)
-            image = x_ref[b].astype(F32)
-            parts = []
-            for j in range(ks):
-                s = j - half
-                if s == 0:
-                    moved = image
-                else:
-                    moved = pltpu.roll(image, (-s) % width, 1)
-                    moved = jnp.where((col + s >= 0) & (col + s < width), moved, 0.0)
-                parts.append(moved.astype(BF16))
-            parts.append(jnp.zeros((lanes - ks * rows_all, width), BF16))
-            moved_all = jnp.concatenate(parts, axis=0)
-            stack[g * PACK + q] = moved_all
-            taps = pltpu.roll(
-                spread, lanes - 8 - 8 * q, 1, stride=1, stride_axis=0
-            )
-            taps = jnp.where(band_mask, taps, 0.0).astype(BF16)
-            out = mm(taps, moved_all)
-            filt[pl.ds(g * PACK + q, rows_all, stride=bp), :] = out.astype(BF16).astype(F32)
-        return 0
-
-    lax.fori_loop(0, groups, filter_group, 0)
+        filt[pl.ds(h * bp + bp - 16, 16), :] = jnp.zeros((16, width), F32)
+
+    place_j = lax.broadcasted_iota(jnp.int32, (ks, lanes), 0)
+    place_l = lax.broadcasted_iota(jnp.int32, (ks, lanes), 1) - (8 - half)
+    base = jnp.zeros((bands, lanes), F32)
+    for i in range(ks):
+        spot = jnp.where(place_l == place_j * rows_all + i, 1.0, 0.0).astype(BF16)
+        base = base + mm_tn(taps_ref[i], spot)
+    tap_rows[0:bands, :] = base
+
+    lower = me_b == 0
+    mid_row = rows_all // 2
+
+    def filter_band(b):
+        image = x_ref[b]
+        parts = []
+        for j in range(ks):
+            s = j - half
+            if s == 0:
+                moved = image
+            else:
+                moved = pltpu.roll(image, (-s) % width, 1)
+                moved = jnp.where((col + s >= 0) & (col + s < width), moved, jnp.zeros((), BF16))
+            parts.append(moved)
+        parts.append(jnp.zeros((lanes - ks * rows_all, width), BF16))
+        moved_all = jnp.concatenate(parts, axis=0)
+        stack[b] = moved_all
+        spread = jnp.broadcast_to(tap_rows[pl.ds(b, 1), :], (rows_all, lanes))
+        taps = pltpu.roll(spread, lanes - 8, 1, stride=1, stride_axis=0)
+        taps = jnp.where(band_mask, taps, 0.0)
+        if split:
+            taps_own[b] = jnp.where(lower, taps[:mid_row], taps[mid_row:]).astype(BF16)
+            taps = jnp.where(lower, taps[mid_row:], taps[:mid_row])
+            first, count = (1 - me_b) * rows, rows
+        else:
+            first, count = 0, rows_all
+        out = mm(taps.astype(BF16), moved_all)
+        filt[pl.ds(first * bp + b, count, stride=bp), :] = out.astype(BF16).astype(F32)
+
+    def filter_own(b):
+        out = mm(taps_own[b], stack[b])
+        filt[pl.ds(me_b * rows * bp + b, rows, stride=bp), :] = out.astype(BF16).astype(F32)
+
+    def over_bands(lo, hi, act):
+        def body(g, _):
+            for q in range(unroll):
+                act(g * unroll + q)
+            return 0
+
+        lax.fori_loop(lo, hi, body, 0)
+
+    groups = bands // unroll
+    over_bands(0, groups, filter_band)
+
+    pick = jnp.where(
+        lax.broadcasted_iota(jnp.int32, (bp, outs), 1)
+        == lax.broadcasted_iota(jnp.int32, (bp, outs), 0) + me_b * bands,
+        1.0, 0.0,
+    )
+    pick = jnp.where(lax.broadcasted_iota(jnp.int32, (bp, outs), 0) < bands, pick, 0.0).astype(BF16)
+    wft_ref[...] = mm_nt(w1t_ref[...], pick).astype(BF16)
 
     def filt_rows(h, count):
         return jnp.concatenate(
@@ -136,8 +176,14 @@
         for c in range(chunks):
             z_part(k, c)
             z_copy(k, c).start()
+    if split:
+        over_bands(0, groups, filter_own)
     for c in range(chunks):
         z_part(0, c)
+    wf_ref[...] = mm_nt(pick, w1t_ref[...]).astype(BF16)
+    wmt_ref[...] = mm_nt(eye(ch), wm_ref[...]).astype(BF16)
+    wot_ref[...] = mm_nt(eye(outs), wo_ref[...]).astype(BF16)
+    wanted[...] = target_ref[...].astype(F32)
 
     def d_copy(k, c):
         part = pl.ds(me_b * rows + c * step_rows, step_rows)
@@ -176,7 +222,7 @@
         for r in range(step_rows):
             h = c * step_rows + r
             factor = (2.0 * scale) * mask_ref[pl.ds(h, 1), :].astype(F32)
-            diff = predicted[:, r * width:(r + 1) * width] - target_ref[h].astype(F32)
+            diff = predicted[:, r * width:(r + 1) * width] - wanted[pl.ds(h, outs, stride=rows), :]
             errs.append((factor * diff).astype(BF16))
         err = wide(errs)
         g_out = g_out + mm_nt(hid_mid, err)
@@ -273,29 +319,22 @@
     skew = lanes - (rows_all - 1) + half
     extra = -skew % 8
     lane_e = jnp.maximum(lane_i - extra, 0)
-    block_e = jnp.where(lane_i >= extra, lane_e // rows_all, ks)
     tap_e = lane_e % rows_all
-
-    def taps_group(g, _):
-        acc = jnp.zeros((rows_all, lanes), F32)
-        for q in range(PACK):
-            b = g * PACK + q
-            rows_b = slope[pl.ds(b, rows_all, stride=bp), :].astype(BF16)
-            cross = mm_nt(rows_b, stack[b])
-            place = 8 * q
-            moved = pltpu.roll(
-                cross, (skew + extra + place) % lanes, 1, stride=1, stride_axis=0
-            )
-            i = tap_e - place
-            source = h_i + i - half
-            valid = (i >= 0) & (i < ks) & (source >= 0) & (source < rows_all) & (block_e < ks)
-            acc = acc + jnp.where(valid, moved, 0.0)
-        summed = jnp.sum(acc, axis=0, keepdims=True)
-        late[pl.ds(g, 1), 0:lanes] = pltpu.roll(summed, lanes - extra, 1)
-        return 0
+    source_e = h_i + tap_e - half
+    valid = (
+        (lane_i >= extra) & (lane_e // rows_all < ks) & (tap_e < ks)
+        & (source_e >= 0) & (source_e < rows_all)
+    )
+    sums[...] = jnp.zeros_like(sums)
+
+    def taps_band(b):
+        rows_b = slope[pl.ds(b, rows_all, stride=bp), :].astype(BF16)
+        cross = mm_nt(rows_b, stack[b])
+        moved = pltpu.roll(cross, (skew + extra) % lanes, 1, stride=1, stride_axis=0)
+        sums[pl.ds(b, 1), :] = jnp.sum(jnp.where(valid, moved, 0.0), axis=0, keepdims=True)
 
     cut = groups // 2
-    lax.fori_loop(0, cut, taps_group, 0)
+    over_bands(0, cut, taps_band)
 
     each(nd, lambda k: scatter_copy(early, early_in, ew, e_ss, e_rs, k).wait_recv())
     own = piece(early, me_d, ew)[...]
@@ -304,7 +343,16 @@
     piece(early_out.at[me_b], me_d, ew)[...] = own
     each(total, lambda k: gather_early(k).start())
 
-    lax.fori_loop(cut, groups, taps_group, 0)
+    over_bands(cut, groups, taps_band)
+
+    slot = (8 * ks, lanes)
+    slot_r = lax.broadcasted_iota(jnp.int32, slot, 0)
+    slot_l = lax.broadcasted_iota(jnp.int32, slot, 1) - extra
+    spot = jnp.where(slot_l == (slot_r % 8) * rows_all + slot_r // 8, 1.0, 0.0)
+    late[0:8 * ks, 0:bp] = lax.dot_general(
+        spot, sums[...], (((1,), (1,)), ((), ())),
+        preferred_element_type=F32, precision=lax.Precision.HIGHEST,
+    )
 
     each(nd, lambda k: scatter_copy(late, late_in, lw, l_ss, l_rs, k).start())
     each(total, lambda k: gather_early(k).wait_recv())
@@ -334,6 +382,15 @@
     each(nd, lambda k: gather_late(k).wait_send())
 
 
+def finish(gk_in, gf_in, gm_in, go_in, gk_out, gf_out, gm_out, go_out):
+    ks, _, bands = gk_out.shape
+    for i in range(ks):
+        gk_out[i] = gk_in[8 * i:8 * i + ks, 0:bands]
+    gf_out[...] = gf_in[...]
+    gm_out[...] = gm_in[...]
+    go_out[...] = go_in[...]
+
+
 def on_device(nd, nb, radiance, kernel_taps, w_first, w_mid, w_out, target, mask):
     image = radiance[0]
     bands, rows_all, width = image.shape
@@ -341,24 +398,21 @@
     ch = w_first.shape[1]
     outs = w_out.shape[1]
     rows = rows_all // nb
-    chunks = 2
-    groups = -(-bands // PACK)
-    bp = up(groups * PACK, 16)
+    chunks = min(4, rows // 2)
+    unroll = max(u for u in range(1, 11) if bands % u == 0)
+    bp = up(bands, 16)
     lane_parts = nd // 8
+    lanes = 8 * rows_all
     ew = up(outs + ch + bands, 128 * lane_parts)
-    lw = up(8 * rows_all, 128 * lane_parts)
+    lw = up(bp, 128 * lane_parts)
     cfg = dict(
-        nd=nd, nb=nb, bands=bands, groups=groups, bp=bp, ks=ks, rows_all=rows_all, rows=rows,
+        nd=nd, nb=nb, bands=bands, unroll=unroll, bp=bp, ks=ks, rows_all=rows_all, rows=rows,
         width=width, chunks=chunks, ch=ch, outs=outs, ew=ew, lw=lw,
         scale=1.0 / math.sqrt(nd * rows_all * width),
     )
-    taps = jnp.pad(kernel_taps, ((0, groups * PACK - bands), (0, 8 - ks), (0, 8 - ks)))
-    taps = taps.reshape(groups, PACK, 8, 8).transpose(0, 3, 1, 2).reshape(groups, 8 * PACK * 8)
-    own = lax.dynamic_slice_in_dim(w_first, lax.axis_index("band") * bands, bands, 0)
-    own = jnp.pad(own, ((0, bp - bands), (0, 0)))
     sems = lambda *shape: pltpu.SemaphoreType.DMA(shape)
-    lanes = 8 * rows_all
-    packed, g_first, g_mid, g_out = pl.pallas_call(
+    vmem = pl.BlockSpec(memory_space=pltpu.VMEM)
+    sums = pl.pallas_call(
         functools.partial(kernel, cfg),
         out_shape=(
             jax.ShapeDtypeStruct((64, lw), F32),
@@ -366,10 +420,18 @@
             jax.ShapeDtypeStruct((ch, ch), F32),
             jax.ShapeDtypeStruct((ch, outs), F32),
         ),
-        in_specs=[pl.BlockSpec(memory_space=pltpu.VMEM)] * 10,
-        out_specs=(pl.BlockSpec(memory_space=pltpu.VMEM),) * 4,
+        in_specs=[vmem] * 7,
+        out_specs=(vmem,) * 4,
         scratch_shapes=[
-            pltpu.VMEM((groups * PACK, lanes, width), BF16),
+            pltpu.VMEM((bp, lanes), F32),
+            pltpu.VMEM((bands, rows_all // 2, lanes), BF16),
+            pltpu.VMEM((ch, bp), BF16),
+            pltpu.VMEM((bp, ch), BF16),
+            pltpu.VMEM((ch, ch), BF16),
+            pltpu.VMEM((outs, ch), BF16),
+            pltpu.VMEM((outs * rows, width), F32),
+            pltpu.VMEM((bp, lanes), F32),
+            pltpu.VMEM((bands, lanes, width), BF16),
             pltpu.VMEM((rows_all * bp, width), F32),
             pltpu.VMEM((rows_all * bp, width), F32),
             pltpu.VMEM((nb, rows, ch, width), F32),
@@ -389,12 +451,21 @@
             collective_id=0, has_side_effects=True, vmem_limit_bytes=56 * 1024 * 1024
         ),
     )(
-        image, taps.astype(F32), own.T, own, w_mid, w_mid.T, w_out, w_out.T,
-        target[0].transpose(1, 0, 2), mask[0],
-    )
-    g_taps = packed[:groups, :lanes].reshape(groups, 8, PACK, 8).transpose(0, 2, 3, 1)
-    g_taps = g_taps.reshape(groups * PACK, 8, 8)[:bands, :ks, :ks]
-    return (g_taps, g_first.T, g_mid, g_out)
+        image, kernel_taps.transpose(1, 2, 0), w_first.T, w_mid, w_out,
+        target[0].reshape(outs * rows, width), mask[0],
+    )
+    g_taps, g_first, g_mid, g_out = pl.pallas_call(
+        finish,
+        out_shape=(
+            jax.ShapeDtypeStruct((ks, ks, bands), F32),
+            jax.ShapeDtypeStruct((ch, bands * nb), F32),
+            jax.ShapeDtypeStruct((ch, ch), F32),
+            jax.ShapeDtypeStruct((ch, outs), F32),
+        ),
+        in_specs=[vmem] * 4,
+        out_specs=(vmem,) * 4,
+    )(*sums)
+    return (g_taps.transpose(2, 0, 1), g_first.T, g_mid, g_out)
 
 
 def solution(mesh):

time: 73.3 us -> 54.3 us (0.74)
  local copies, waits for them, and re-layouts: 11.8 us -> 0 us
  Pallas kernels: 59.7 us -> 53.4 us
  other arithmetic: 0.75 us -> 0 us
    pallas_call x1, Pallas kernels: 59.7 us -> 51.7 us  [on_device(): pl.pallas_call(functools.partial(kernel, cfg), out_shape=(jax.ShapeDtypeS...]
    unnamed x18 -> x0, local copies, waits for them, and re-layouts: 7.32 us -> none
    pallas_call x0 -> x1, Pallas kernels: none -> 1.71 us  [on_device(): pl.pallas_call(finish, out_shape=(jax.ShapeDtypeStruct((ks, ks, bands), F...]
    convert_element_type x3 -> x0, local copies, waits for them, and re-layouts: 1.54 us -> none  [on_device(): taps.astype(F32)]
    transpose x2 -> x0, local copies, waits for them, and re-layouts: 1.27 us -> none  [the longest x1 0.71 us: on_device(): packed, g_first, g_mid, g_out = pl.pallas_call(functools.partial(kernel,...]
    slice x2 -> x0, local copies, waits for them, and re-layouts: 0.94 us -> none  [on_device(): packed[:groups, :lanes].reshape(groups, 8, PACK, 8).transpose(0, 2, 3, 1)]
    convert_element_type x1 -> x0, other arithmetic: 0.75 us -> none  [on_device(): taps.astype(F32)]
where the time goes in v2:
time: 54.3 us; the launch traced here: 54.1 us
  Pallas kernels  53.4 us (98%)
  between operations  0.64 us (1%)
    pallas_call x1, Pallas kernels, on_device(): pl.pallas_call(functools.partial(kernel, cfg), out_shape=(jax.ShapeDtypeS...  51.7 us
    pallas_call x1, Pallas kernels, on_device(): pl.pallas_call(finish, out_shape=(jax.ShapeDtypeStruct((ks, ks, bands), F...  1.71 us

profile of v2, /device:TPU:0, one launch (start us, length us, event | category | flops | bytes accessed | tf_op | source)
XLA Modules:
  0.0 54.1 jit_solution(962243809240900628)
XLA Ops:
  0.6 51.7 %shard_map.102 = (f32[64,256]{1,0:T(8,128)}, f32[64,280]{1,0:T(8,128)}, f32[64,64]{1,0:T(8,128)}, f32[64,280]{1,0:T(8,128)}) custom-call(bf16[140,32,128]{2,1,0:T(8,128)(2,1)} %bitcast.7, bf16[7,7,140]{2,1,0:T(8,128)(2,1)} %bitcast.10, bf16[64,280]{1,0:T(8,128)(2,1)} %bitcast.9, bf16[64,64]{1,0:T(8,128)(2,1)} %wm_ref.1, bf16[64,280]{1,0:T(8,128)(2,1)} %wo_ref.1, ...), custom_call_target="tpu_custom_call" | custom-call | tf_op jit(solution)/shard_map/pallas_call | solution.py:415
  52.4 1.7 %shard_map.103 = (f32[7,7,140]{2,1,0:T(8,128)}, f32[64,280]{1,0:T(8,128)}, f32[64,64]{1,0:T(8,128)}, f32[64,280]{1,0:T(8,128)}) custom-call(f32[64,256]{1,0:T(8,128)} %get-tuple-element.12.gk_in, f32[64,280]{1,0:T(8,128)} %get-tuple-element.13.gf_in, f32[64,64]{1,0:T(8,128)} %get-tuple-element.14.gm_in, f32[64,280]{1,0:T(8,128)} %get-tuple-element.15.go_in), custom_call_target="tpu_custom_call" | custom-call | tf_op jit(solution)/shard_map/pallas_call | solution.py:457

commit v3 on v2

--- a/solution.py
+++ b/solution.py
@@ -39,14 +39,16 @@
     x_ref, taps_ref, w1t_ref, wm_ref, wo_ref, target_ref, mask_ref,
     gk_ref, gf_ref, gm_ref, go_ref,
     tap_rows, taps_own, wft_ref, wf_ref, wmt_ref, wot_ref, wanted, sums, stack, filt, slope, z_send, z_recv, dz_all, hid_s,
-    early, early_in, early_out, late, late_in,
-    z_ss, z_rs, d_ss, d_rs, e_ss, e_rs, ea_ss, ea_rs, l_ss, l_rs, la_ss, la_rs,
+    early, early_in, early_x, early_out, first_g, first_in, first_out, late, late_in,
+    z_ss, z_rs, d_ss, d_rs, e_ss, e_rs, ex_ss, ex_rs, ea_ss, ea_rs,
+    f_ss, f_rs, fa_ss, fa_rs, l_ss, l_rs, la_ss, la_rs,
 ):
     nd, nb = cfg["nd"], cfg["nb"]
     bands, unroll, bp, ks = cfg["bands"], cfg["unroll"], cfg["bp"], cfg["ks"]
+    fs, ts = cfg["fs"], cfg["ts"]
     rows_all, rows, width, chunks = cfg["rows_all"], cfg["rows"], cfg["width"], cfg["chunks"]
     ch, outs, scale = cfg["ch"], cfg["outs"], cfg["scale"]
-    ew, lw = cfg["ew"], cfg["lw"]
+    ew, gw, lw = cfg["ew"], cfg["gw"], cfg["lw"]
     half = ks // 2
     lanes = 8 * rows_all
     step_rows = rows // chunks
@@ -76,7 +78,7 @@
     band_mask = (tap >= 0) & (tap < ks) & (block < ks)
     col = lax.broadcasted_iota(jnp.int32, (rows_all, width), 1)
     for h in range(rows_all):
-        filt[pl.ds(h * bp + bp - 16, 16), :] = jnp.zeros((16, width), F32)
+        filt[pl.ds(h * fs + bp - 16, 16), :] = jnp.zeros((16, width), F32)
 
     place_j = lax.broadcasted_iota(jnp.int32, (ks, lanes), 0)
     place_l = lax.broadcasted_iota(jnp.int32, (ks, lanes), 1) - (8 - half)
@@ -113,11 +115,11 @@
         else:
             first, count = 0, rows_all
         out = mm(taps.astype(BF16), moved_all)
-        filt[pl.ds(first * bp + b, count, stride=bp), :] = out.astype(BF16).astype(F32)
+        filt[pl.ds(first * fs + b, count, stride=fs), :] = out.astype(BF16).astype(F32)
 
     def filter_own(b):
         out = mm(taps_own[b], stack[b])
-        filt[pl.ds(me_b * rows * bp + b, rows, stride=bp), :] = out.astype(BF16).astype(F32)
+        filt[pl.ds(me_b * rows * fs + b, rows, stride=fs), :] = out.astype(BF16).astype(F32)
 
     def over_bands(lo, hi, act):
         def body(g, _):
@@ -141,7 +143,7 @@
     def filt_rows(h, count):
         return jnp.concatenate(
             [
-                filt[pl.ds(pl.multiple_of((h + r) * bp, 8), bp), :].astype(BF16)
+                filt[pl.ds(pl.multiple_of((h + r) * fs, 8), bp), :].astype(BF16)
                 for r in range(count)
             ],
             axis=1,
@@ -183,7 +185,17 @@
     wf_ref[...] = mm_nt(pick, w1t_ref[...]).astype(BF16)
     wmt_ref[...] = mm_nt(eye(ch), wm_ref[...]).astype(BF16)
     wot_ref[...] = mm_nt(eye(outs), wo_ref[...]).astype(BF16)
-    wanted[...] = target_ref[...].astype(F32)
+    if ts == rows:
+        wanted[...] = target_ref[...].astype(F32)
+    else:
+        def widen(g, _):
+            for q in range(8):
+                o = g * 8 + q
+                block_o = target_ref[pl.ds(pl.multiple_of(o * rows, 16), rows), :]
+                wanted[pl.ds(pl.multiple_of(o * ts, 8), rows), :] = block_o.astype(F32)
+            return 0
+
+        lax.fori_loop(0, outs // 8, widen, 0)
 
     def d_copy(k, c):
         part = pl.ds(me_b * rows + c * step_rows, step_rows)
@@ -222,7 +234,7 @@
         for r in range(step_rows):
             h = c * step_rows + r
             factor = (2.0 * scale) * mask_ref[pl.ds(h, 1), :].astype(F32)
-            diff = predicted[:, r * width:(r + 1) * width] - wanted[pl.ds(h, outs, stride=rows), :]
+            diff = predicted[:, r * width:(r + 1) * width] - wanted[pl.ds(h, outs, stride=ts), :]
             errs.append((factor * diff).astype(BF16))
         err = wide(errs)
         g_out = g_out + mm_nt(hid_mid, err)
@@ -237,35 +249,12 @@
         for k in range(1, nb):
             d_copy(k, c).start()
 
-    hid_s[...] = jnp.zeros_like(hid_s)
-
-    def slope_rows(first):
-        def one(p, _):
-            h = first + 2 * p
-            dz = wide([dz_all[h], dz_all[h + 1]])
-            hid_s[...] += mm_nt(dz, filt_rows(h, 2))
-            back = mm(wf_ref[...], dz)
-            for r in range(2):
-                place = pl.multiple_of((rows_all - 1 - h - r) * bp, 8)
-                slope[pl.ds(place, bp), :] = back[:, r * width:(r + 1) * width]
-            return 0
-
-        lax.fori_loop(0, step_rows // 2, one, 0, unroll=True)
-
-    for c in range(chunks):
-        slope_rows(me_b * rows + c * step_rows)
-    for k in range(1, nb):
-        source = lax.rem(me_b + nb - k, nb)
-        for c in range(chunks):
-            d_copy(k, c).wait_recv()
-            slope_rows(source * rows + c * step_rows)
-
     def piece(ref, index, w):
         lane_parts = nd // 8
-        each = w // lane_parts
+        each_w = w // lane_parts
         return ref.at[
             pl.ds(pl.multiple_of((index // lane_parts) * 8, 8), 8),
-            pl.ds(pl.multiple_of(lax.rem(index, lane_parts) * each, 128), each),
+            pl.ds(pl.multiple_of(lax.rem(index, lane_parts) * each_w, 128), each_w),
         ]
 
     def scatter_copy(ref, into, w, ss, rs, k):
@@ -279,6 +268,17 @@
             device_id_type=MESH,
         )
 
+    def gather_copy(ref, w, ss, rs, device_of, k):
+        part = piece(ref, me_d, w)
+        return pltpu.make_async_remote_copy(
+            src_ref=part,
+            dst_ref=part,
+            send_sem=ss.at[k],
+            recv_sem=rs.at[k],
+            device_id=device_of(k),
+            device_id_type=MESH,
+        )
+
     def each(count, act):
         def body(k, _):
             act(k)
@@ -286,99 +286,164 @@
 
         lax.fori_loop(1, count, body, 0)
 
+    def crop_peer(k):
+        return (lax.rem(me_d + k, nd), me_b)
+
+    def any_peer(k):
+        return device(lax.rem(me + k, total))
+
+    def add_up(ref, into, w):
+        own = piece(ref, me_d, w)[...]
+        for k in range(1, nd):
+            own = own + into[k]
+        return own
+
+    def scatter_early(k):
+        return scatter_copy(early, early_in, ew, e_ss, e_rs, k)
+
+    def band_early(k):
+        return pltpu.make_async_remote_copy(
+            src_ref=early_x.at[0],
+            dst_ref=early_x.at[k],
+            send_sem=ex_ss.at[k],
+            recv_sem=ex_rs.at[k],
+            device_id=(me_d, lax.rem(me_b + k, nb)),
+            device_id_type=MESH,
+        )
+
     def gather_early(k):
-        part = piece(early_out.at[me_b], me_d, ew)
-        return pltpu.make_async_remote_copy(
-            src_ref=part,
-            dst_ref=part,
-            send_sem=ea_ss.at[k],
-            recv_sem=ea_rs.at[k],
-            device_id=device(lax.rem(me + k, total)),
-            device_id_type=MESH,
-        )
+        return gather_copy(early_out, ew, ea_ss, ea_rs, crop_peer, k)
+
+    def scatter_first(k):
+        return scatter_copy(first_g, first_in, gw, f_ss, f_rs, k)
+
+    def gather_first(k):
+        return gather_copy(first_out.at[me_b], gw, fa_ss, fa_rs, any_peer, k)
+
+    def scatter_late(k):
+        return scatter_copy(late, late_in, lw, l_ss, l_rs, k)
 
     def gather_late(k):
-        part = piece(gk_ref, me_d, lw)
-        return pltpu.make_async_remote_copy(
-            src_ref=part,
-            dst_ref=part,
-            send_sem=la_ss.at[k],
-            recv_sem=la_rs.at[k],
-            device_id=(lax.rem(me_d + k, nd), me_b),
-            device_id_type=MESH,
-        )
+        return gather_copy(gk_ref, lw, la_ss, la_rs, crop_peer, k)
 
     early[...] = jnp.zeros_like(early)
     early[:, 0:outs] = g_out
     early[:, outs:outs + ch] = g_mid
-    early[:, outs + ch:outs + ch + bands] = hid_s[:, 0:bands]
-    each(nd, lambda k: scatter_copy(early, early_in, ew, e_ss, e_rs, k).start())
+    each(nd, lambda k: scatter_early(k).start())
+    first_g[...] = jnp.zeros_like(first_g)
     late[...] = jnp.zeros_like(late)
-
-    h_i = rows_all - 1 - row_i
+    sums[...] = jnp.zeros_like(sums)
+
+    hid_s[...] = jnp.zeros_like(hid_s)
+
+    def slope_rows(first):
+        def one(p, _):
+            h = first + 2 * p
+            dz = wide([dz_all[h], dz_all[h + 1]])
+            hid_s[...] += mm_nt(dz, filt_rows(h, 2))
+            back = mm(wf_ref[...], dz)
+            for r in range(2):
+                place = pl.multiple_of((rows_all - 1 - h - r) * fs, 8)
+                slope[pl.ds(place, bp), :] = back[:, r * width:(r + 1) * width]
+            return 0
+
+        lax.fori_loop(0, step_rows // 2, one, 0, unroll=True)
+
     skew = lanes - (rows_all - 1) + half
     extra = -skew % 8
-    lane_e = jnp.maximum(lane_i - extra, 0)
-    tap_e = lane_e % rows_all
-    source_e = h_i + tap_e - half
-    valid = (
-        (lane_i >= extra) & (lane_e // rows_all < ks) & (tap_e < ks)
-        & (source_e >= 0) & (source_e < rows_all)
-    )
-    sums[...] = jnp.zeros_like(sums)
-
-    def taps_band(b):
-        rows_b = slope[pl.ds(b, rows_all, stride=bp), :].astype(BF16)
-        cross = mm_nt(rows_b, stack[b])
-        moved = pltpu.roll(cross, (skew + extra) % lanes, 1, stride=1, stride_axis=0)
-        sums[pl.ds(b, 1), :] = jnp.sum(jnp.where(valid, moved, 0.0), axis=0, keepdims=True)
-
+
+    def taps_part(part, start, count, lo, hi):
+        lane = lax.broadcasted_iota(jnp.int32, (count, lanes), 1)
+        row = lax.broadcasted_iota(jnp.int32, (count, lanes), 0)
+        lane = lax.rem(lane + start + (lanes - extra), lanes)
+        tap_e = lane % rows_all
+        source = rows_all - 1 - start - row + tap_e - half
+        valid = (lane < ks * rows_all) & (tap_e < ks) & (source >= 0) & (source < rows_all)
+
+        def taps_band(b):
+            rows_b = slope[pl.ds(start * fs + b, count, stride=fs), :].astype(BF16)
+            cross = mm_nt(rows_b, stack[b])
+            moved = pltpu.roll(cross, (skew + extra) % lanes, 1, stride=1, stride_axis=0)
+            moved = jnp.where(valid, moved, 0.0)
+            sums[part, pl.ds(b, 1), :] = jnp.sum(moved, axis=0, keepdims=True)
+
+        over_bands(lo, hi, taps_band)
+
+    for c in range(chunks):
+        slope_rows(me_b * rows + c * step_rows)
+    if split:
+        taps_part(0, (1 - me_b) * rows, rows, 0, groups)
+
+    each(nd, lambda k: scatter_early(k).wait_recv())
+    early_x[0] = add_up(early, early_in, ew)
+    for k in range(1, nb):
+        band_early(k).start()
+
+    for k in range(1, nb):
+        source = lax.rem(me_b + nb - k, nb)
+        for c in range(chunks):
+            d_copy(k, c).wait_recv()
+            slope_rows(source * rows + c * step_rows)
+
+    first_g[:, 0:bp] = hid_s[...]
+    each(nd, lambda k: scatter_first(k).start())
+    own = early_x[0]
+    for k in range(1, nb):
+        band_early(k).wait_recv()
+        own = own + early_x[k]
+    piece(early_out, me_d, ew)[...] = own
+    each(nd, lambda k: gather_early(k).start())
+
+    rest = (me_b * rows, rows) if split else (0, rows_all)
     cut = groups // 2
-    over_bands(0, cut, taps_band)
-
-    each(nd, lambda k: scatter_copy(early, early_in, ew, e_ss, e_rs, k).wait_recv())
-    own = piece(early, me_d, ew)[...]
-    for k in range(1, nd):
-        own = own + early_in[k]
-    piece(early_out.at[me_b], me_d, ew)[...] = own
-    each(total, lambda k: gather_early(k).start())
-
-    over_bands(cut, groups, taps_band)
-
-    slot = (8 * ks, lanes)
-    slot_r = lax.broadcasted_iota(jnp.int32, slot, 0)
-    slot_l = lax.broadcasted_iota(jnp.int32, slot, 1) - extra
-    spot = jnp.where(slot_l == (slot_r % 8) * rows_all + slot_r // 8, 1.0, 0.0)
-    late[0:8 * ks, 0:bp] = lax.dot_general(
-        spot, sums[...], (((1,), (1,)), ((), ())),
-        preferred_element_type=F32, precision=lax.Precision.HIGHEST,
-    )
-
-    each(nd, lambda k: scatter_copy(late, late_in, lw, l_ss, l_rs, k).start())
-    each(total, lambda k: gather_early(k).wait_recv())
-    result = early_out[0]
+    taps_part(1, *rest, 0, cut)
+
+    each(nd, lambda k: scatter_first(k).wait_recv())
+    piece(first_out.at[me_b], me_d, gw)[...] = add_up(first_g, first_in, gw)
+    each(total, lambda k: gather_first(k).start())
+
+    taps_part(1, *rest, cut, groups)
+
+    def pick_taps(part, start):
+        slot = (8 * ks, lanes)
+        r = lax.broadcasted_iota(jnp.int32, slot, 0)
+        lane = lax.broadcasted_iota(jnp.int32, slot, 1)
+        lane = lax.rem(lane + start + (lanes - extra), lanes)
+        spot = jnp.where(lane == (r % 8) * rows_all + r // 8, 1.0, 0.0)
+        return lax.dot_general(
+            spot, sums[part], (((1,), (1,)), ((), ())),
+            preferred_element_type=F32, precision=lax.Precision.HIGHEST,
+        )
+
+    taps_sum = pick_taps(1, rest[0])
+    if split:
+        taps_sum = taps_sum + pick_taps(0, (1 - me_b) * rows)
+    late[0:8 * ks, 0:bp] = taps_sum
+    each(nd, lambda k: scatter_late(k).start())
+
+    each(nd, lambda k: gather_early(k).wait_recv())
+    go_ref[...] = early_out[:, 0:outs]
+    gm_ref[...] = early_out[:, outs:outs + ch]
+
+    each(nd, lambda k: scatter_late(k).wait_recv())
+    piece(gk_ref, me_d, lw)[...] = add_up(late, late_in, lw)
+    each(nd, lambda k: gather_late(k).start())
+
+    each(total, lambda k: gather_first(k).wait_recv())
+    for k in range(nb):
+        gf_ref[:, k * bands:(k + 1) * bands] = first_out[k, :, 0:bands]
+    each(nd, lambda k: gather_late(k).wait_recv())
+
     for k in range(1, nb):
-        result = result + early_out[k]
-    go_ref[...] = result[:, 0:outs]
-    gm_ref[...] = result[:, outs:outs + ch]
-    for k in range(nb):
-        gf_ref[:, k * bands:(k + 1) * bands] = early_out[k, :, outs + ch:outs + ch + bands]
-
-    each(nd, lambda k: scatter_copy(late, late_in, lw, l_ss, l_rs, k).wait_recv())
-    own = piece(late, me_d, lw)[...]
-    for k in range(1, nd):
-        own = own + late_in[k]
-    piece(gk_ref, me_d, lw)[...] = own
-    each(nd, lambda k: gather_late(k).start())
-    each(nd, lambda k: gather_late(k).wait_recv())
-
-    for k in range(1, nb):
+        band_early(k).wait_send()
         for c in range(chunks):
             z_copy(k, c).wait_send()
             d_copy(k, c).wait_send()
-    each(nd, lambda k: scatter_copy(early, early_in, ew, e_ss, e_rs, k).wait_send())
-    each(total, lambda k: gather_early(k).wait_send())
-    each(nd, lambda k: scatter_copy(late, late_in, lw, l_ss, l_rs, k).wait_send())
+    each(nd, lambda k: scatter_early(k).wait_send())
+    each(nd, lambda k: gather_early(k).wait_send())
+    each(nd, lambda k: scatter_first(k).wait_send())
+    each(total, lambda k: gather_first(k).wait_send())
+    each(nd, lambda k: scatter_late(k).wait_send())
     each(nd, lambda k: gather_late(k).wait_send())
 
 
@@ -401,13 +466,16 @@
     chunks = min(4, rows // 2)
     unroll = max(u for u in range(1, 11) if bands % u == 0)
     bp = up(bands, 16)
+    fs = bp + 8
+    ts = rows + 8 if rows % 16 == 0 and outs % 8 == 0 else rows
     lane_parts = nd // 8
     lanes = 8 * rows_all
-    ew = up(outs + ch + bands, 128 * lane_parts)
+    ew = up(outs + ch, 128 * lane_parts)
+    gw = up(bp, 128 * lane_parts)
     lw = up(bp, 128 * lane_parts)
     cfg = dict(
         nd=nd, nb=nb, bands=bands, unroll=unroll, bp=bp, ks=ks, rows_all=rows_all, rows=rows,
-        width=width, chunks=chunks, ch=ch, outs=outs, ew=ew, lw=lw,
+        width=width, chunks=chunks, ch=ch, outs=outs, ew=ew, gw=gw, lw=lw, fs=fs, ts=ts,
         scale=1.0 / math.sqrt(nd * rows_all * width),
     )
     sems = lambda *shape: pltpu.SemaphoreType.DMA(shape)
@@ -429,21 +497,26 @@
             pltpu.VMEM((bp, ch), BF16),
             pltpu.VMEM((ch, ch), BF16),
             pltpu.VMEM((outs, ch), BF16),
-            pltpu.VMEM((outs * rows, width), F32),
-            pltpu.VMEM((bp, lanes), F32),
+            pltpu.VMEM((outs * ts, width), F32),
+            pltpu.VMEM((2, bp, lanes), F32),
             pltpu.VMEM((bands, lanes, width), BF16),
-            pltpu.VMEM((rows_all * bp, width), F32),
-            pltpu.VMEM((rows_all * bp, width), F32),
+            pltpu.VMEM((rows_all * fs, width), F32),
+            pltpu.VMEM((rows_all * fs, width), F32),
             pltpu.VMEM((nb, rows, ch, width), F32),
             pltpu.VMEM((nb, rows, ch, width), F32),
             pltpu.VMEM((rows_all, ch, width), BF16),
             pltpu.VMEM((ch, bp), F32),
             pltpu.VMEM((64, ew), F32),
             pltpu.VMEM((nd, 8, ew // lane_parts), F32),
-            pltpu.VMEM((nb, 64, ew), F32),
+            pltpu.VMEM((nb, 8, ew // lane_parts), F32),
+            pltpu.VMEM((64, ew), F32),
+            pltpu.VMEM((64, gw), F32),
+            pltpu.VMEM((nd, 8, gw // lane_parts), F32),
+            pltpu.VMEM((nb, 64, gw), F32),
             pltpu.VMEM((64, lw), F32),
             pltpu.VMEM((nd, 8, lw // lane_parts), F32),
             sems(nb, chunks), sems(nb, chunks), sems(nb, chunks), sems(nb, chunks),
+            sems(nd), sems(nd), sems(nb), sems(nb), sems(nd), sems(nd),
             sems(nd), sems(nd), sems(nd * nb), sems(nd * nb),
             sems(nd), sems(nd), sems(nd), sems(nd),
         ],

time: 54.3 us -> 55.9 us (1.029)
  Pallas kernels: 53.4 us -> 55.1 us
    pallas_call x1, Pallas kernels: 51.7 us -> 53.4 us  [on_device(): pl.pallas_call(functools.partial(kernel, cfg), out_shape=(jax.ShapeDtypeS...]
where the time goes in v3:
time: 55.9 us; the launch traced here: 55.8 us
  Pallas kernels  55.1 us (99%)
  between operations  0.64 us (1%)
    pallas_call x1, Pallas kernels, on_device(): pl.pallas_call(functools.partial(kernel, cfg), out_shape=(jax.ShapeDtypeS...  53.4 us
    pallas_call x1, Pallas kernels, on_device(): pl.pallas_call(finish, out_shape=(jax.ShapeDtypeStruct((ks, ks, bands), F...  1.71 us

profile of v3, /device:TPU:0, one launch (start us, length us, event | category | flops | bytes accessed | tf_op | source)
XLA Modules:
  0.0 55.8 jit_solution(12511215263935405386)
XLA Ops:
  0.6 53.4 %shard_map.102 = (f32[64,256]{1,0:T(8,128)}, f32[64,280]{1,0:T(8,128)}, f32[64,64]{1,0:T(8,128)}, f32[64,280]{1,0:T(8,128)}) custom-call(bf16[140,32,128]{2,1,0:T(8,128)(2,1)} %bitcast.7, bf16[7,7,140]{2,1,0:T(8,128)(2,1)} %bitcast.10, bf16[64,280]{1,0:T(8,128)(2,1)} %bitcast.9, bf16[64,64]{1,0:T(8,128)(2,1)} %wm_ref.1, bf16[64,280]{1,0:T(8,128)(2,1)} %wo_ref.1, ...), custom_call_target="tpu_custom_call" | custom-call | tf_op jit(solution)/shard_map/pallas_call | solution.py:483
  54.1 1.7 %shard_map.103 = (f32[7,7,140]{2,1,0:T(8,128)}, f32[64,280]{1,0:T(8,128)}, f32[64,64]{1,0:T(8,128)}, f32[64,280]{1,0:T(8,128)}) custom-call(f32[64,256]{1,0:T(8,128)} %get-tuple-element.12.gk_in, f32[64,280]{1,0:T(8,128)} %get-tuple-element.13.gf_in, f32[64,64]{1,0:T(8,128)} %get-tuple-element.14.gm_in, f32[64,280]{1,0:T(8,128)} %get-tuple-element.15.go_in), custom_call_target="tpu_custom_call" | custom-call | tf_op jit(solution)/shard_map/pallas_call | solution.py:530

commit v4 on v3

--- a/solution.py
+++ b/solution.py
@@ -38,45 +38,58 @@
     cfg,
     x_ref, taps_ref, w1t_ref, wm_ref, wo_ref, target_ref, mask_ref,
     gk_ref, gf_ref, gm_ref, go_ref,
-    tap_rows, taps_own, wft_ref, wf_ref, wmt_ref, wot_ref, wanted, sums, stack, filt, slope, z_send, z_recv, dz_all, hid_s,
-    early, early_in, early_x, early_out, first_g, first_in, first_out, late, late_in,
-    z_ss, z_rs, d_ss, d_rs, e_ss, e_rs, ex_ss, ex_rs, ea_ss, ea_rs,
-    f_ss, f_rs, fa_ss, fa_rs, l_ss, l_rs, la_ss, la_rs,
+    band_mask, edge, diag_mask, tap_rows, taps_own, wft_ref, wf_ref, wmt_ref, wot_ref, wanted, sums, stack, filt, slope, z_send, z_recv, dz_all, hid_s,
+    early, early_in, early_out, total_ref, sides, late, late_in, late_out,
+    z_ss, z_rs, d_ss, d_rs, ex_ss, ex_rs, e_ss, e_rs, ea_ss, ea_rs, l_ss, l_rs, la_ss, la_rs,
 ):
     nd, nb = cfg["nd"], cfg["nb"]
     bands, unroll, bp, ks = cfg["bands"], cfg["unroll"], cfg["bp"], cfg["ks"]
     fs, ts = cfg["fs"], cfg["ts"]
     rows_all, rows, width, chunks = cfg["rows_all"], cfg["rows"], cfg["width"], cfg["chunks"]
     ch, outs, scale = cfg["ch"], cfg["outs"], cfg["scale"]
-    ew, gw, lw = cfg["ew"], cfg["gw"], cfg["lw"]
+    ew, lw = cfg["ew"], cfg["lw"]
     half = ks // 2
     lanes = 8 * rows_all
     step_rows = rows // chunks
     me_d = lax.axis_index("dp")
     me_b = lax.axis_index("band")
-    me = me_d * nb + me_b
-    total = nd * nb
     split = nb == 2
 
-    def device(index):
-        return (index // nb, lax.rem(index, nb))
+    def each(count, act):
+        if count <= 16:
+            for k in range(1, count):
+                act(k)
+            return
+
+        def body(k, _):
+            act(k)
+            return 0
+
+        lax.fori_loop(1, count, body, 0)
+
+    def crop_peer(k):
+        return (lax.rem(me_d + k, nd), me_b)
+
+    def band_peer(k):
+        return (me_d, lax.rem(me_b + k, nb))
 
     barrier = pltpu.get_barrier_semaphore()
 
-    def greet(k, _):
-        pl.semaphore_signal(
-            barrier, inc=1, device_id=device(lax.rem(me + k, total)), device_id_type=MESH
-        )
-        return 0
-
-    lax.fori_loop(1, total, greet, 0)
+    def greet(peer):
+        pl.semaphore_signal(barrier, inc=1, device_id=peer, device_id_type=MESH)
+
+    each(nd, lambda k: greet(crop_peer(k)))
+    each(nb, lambda k: greet(band_peer(k)))
 
     row_i = lax.broadcasted_iota(jnp.int32, (rows_all, lanes), 0)
     lane_i = lax.broadcasted_iota(jnp.int32, (rows_all, lanes), 1)
     block = lane_i // rows_all
     tap = lane_i % rows_all - row_i + half
-    band_mask = (tap >= 0) & (tap < ks) & (block < ks)
+    band_mask[...] = jnp.where((tap >= 0) & (tap < ks) & (block < ks), 1.0, 0.0)
     col = lax.broadcasted_iota(jnp.int32, (rows_all, width), 1)
+    for j in range(ks):
+        inside = (col + (j - half) >= 0) & (col + (j - half) < width)
+        edge[j] = jnp.where(inside, 1.0, 0.0).astype(BF16)
     for h in range(rows_all):
         filt[pl.ds(h * fs + bp - 16, 16), :] = jnp.zeros((16, width), F32)
 
@@ -99,15 +112,14 @@
             if s == 0:
                 moved = image
             else:
-                moved = pltpu.roll(image, (-s) % width, 1)
-                moved = jnp.where((col + s >= 0) & (col + s < width), moved, jnp.zeros((), BF16))
+                moved = pltpu.roll(image, (-s) % width, 1) * edge[j]
             parts.append(moved)
         parts.append(jnp.zeros((lanes - ks * rows_all, width), BF16))
         moved_all = jnp.concatenate(parts, axis=0)
         stack[b] = moved_all
         spread = jnp.broadcast_to(tap_rows[pl.ds(b, 1), :], (rows_all, lanes))
         taps = pltpu.roll(spread, lanes - 8, 1, stride=1, stride_axis=0)
-        taps = jnp.where(band_mask, taps, 0.0)
+        taps = taps * band_mask[...]
         if split:
             taps_own[b] = jnp.where(lower, taps[:mid_row], taps[mid_row:]).astype(BF16)
             taps = jnp.where(lower, taps[mid_row:], taps[:mid_row])
@@ -149,7 +161,7 @@
             axis=1,
         )
 
-    pl.semaphore_wait(barrier, total - 1)
+    pl.semaphore_wait(barrier, nd + nb - 2)
 
     def z_copy(k, c):
         part = pl.ds(c * step_rows, step_rows)
@@ -257,40 +269,28 @@
             pl.ds(pl.multiple_of(lax.rem(index, lane_parts) * each_w, 128), each_w),
         ]
 
-    def scatter_copy(ref, into, w, ss, rs, k):
-        peer = lax.rem(me_d + k, nd)
+    def remote(src, dst, ss, rs, peer):
         return pltpu.make_async_remote_copy(
-            src_ref=piece(ref, peer, w),
-            dst_ref=into.at[k],
-            send_sem=ss.at[k],
-            recv_sem=rs.at[k],
-            device_id=(peer, me_b),
-            device_id_type=MESH,
+            src_ref=src, dst_ref=dst, send_sem=ss, recv_sem=rs,
+            device_id=peer, device_id_type=MESH,
         )
 
-    def gather_copy(ref, w, ss, rs, device_of, k):
-        part = piece(ref, me_d, w)
-        return pltpu.make_async_remote_copy(
-            src_ref=part,
-            dst_ref=part,
-            send_sem=ss.at[k],
-            recv_sem=rs.at[k],
-            device_id=device_of(k),
-            device_id_type=MESH,
-        )
-
-    def each(count, act):
-        def body(k, _):
-            act(k)
-            return 0
-
-        lax.fori_loop(1, count, body, 0)
-
-    def crop_peer(k):
-        return (lax.rem(me_d + k, nd), me_b)
-
-    def any_peer(k):
-        return device(lax.rem(me + k, total))
+    def scatter(ref, into, w, ss, rs):
+        def start(k):
+            peer = crop_peer(k)
+            remote(piece(ref, peer[0], w), into.at[k], ss, rs, peer).start()
+
+        each(nd, start)
+
+    def gather(out, ss, rs):
+        def start(k):
+            remote(out.at[me_d], out.at[me_d], ss, rs, crop_peer(k)).start()
+
+        each(nd, start)
+
+    def wait_all(ref, sem):
+        rest = ref.at[pl.ds(1, nd - 1)]
+        pltpu.make_async_copy(rest, rest, sem).wait()
 
     def add_up(ref, into, w):
         own = piece(ref, me_d, w)[...]
@@ -298,39 +298,18 @@
             own = own + into[k]
         return own
 
-    def scatter_early(k):
-        return scatter_copy(early, early_in, ew, e_ss, e_rs, k)
-
     def band_early(k):
-        return pltpu.make_async_remote_copy(
-            src_ref=early_x.at[0],
-            dst_ref=early_x.at[k],
-            send_sem=ex_ss.at[k],
-            recv_sem=ex_rs.at[k],
-            device_id=(me_d, lax.rem(me_b + k, nb)),
-            device_id_type=MESH,
+        return remote(
+            early_out.at[me_d, me_b], early_out.at[me_d, me_b], ex_ss.at[k], ex_rs.at[k], band_peer(k)
         )
 
-    def gather_early(k):
-        return gather_copy(early_out, ew, ea_ss, ea_rs, crop_peer, k)
-
-    def scatter_first(k):
-        return scatter_copy(first_g, first_in, gw, f_ss, f_rs, k)
-
-    def gather_first(k):
-        return gather_copy(first_out.at[me_b], gw, fa_ss, fa_rs, any_peer, k)
-
-    def scatter_late(k):
-        return scatter_copy(late, late_in, lw, l_ss, l_rs, k)
-
-    def gather_late(k):
-        return gather_copy(gk_ref, lw, la_ss, la_rs, crop_peer, k)
+    def spread_out(out, w, put):
+        lane_parts = nd // 8
+        each_w = w // lane_parts
+        for d in range(nd):
+            put(out, d, (d // lane_parts) * 8, (d % lane_parts) * each_w, each_w)
 
     early[...] = jnp.zeros_like(early)
-    early[:, 0:outs] = g_out
-    early[:, outs:outs + ch] = g_mid
-    each(nd, lambda k: scatter_early(k).start())
-    first_g[...] = jnp.zeros_like(first_g)
     late[...] = jnp.zeros_like(late)
     sums[...] = jnp.zeros_like(sums)
 
@@ -352,99 +331,102 @@
     skew = lanes - (rows_all - 1) + half
     extra = -skew % 8
 
-    def taps_part(part, start, count, lo, hi):
-        lane = lax.broadcasted_iota(jnp.int32, (count, lanes), 1)
-        row = lax.broadcasted_iota(jnp.int32, (count, lanes), 0)
-        lane = lax.rem(lane + start + (lanes - extra), lanes)
-        tap_e = lane % rows_all
-        source = rows_all - 1 - start - row + tap_e - half
-        valid = (lane < ks * rows_all) & (tap_e < ks) & (source >= 0) & (source < rows_all)
-
-        def taps_band(b):
-            rows_b = slope[pl.ds(start * fs + b, count, stride=fs), :].astype(BF16)
-            cross = mm_nt(rows_b, stack[b])
-            moved = pltpu.roll(cross, (skew + extra) % lanes, 1, stride=1, stride_axis=0)
-            moved = jnp.where(valid, moved, 0.0)
-            sums[part, pl.ds(b, 1), :] = jnp.sum(moved, axis=0, keepdims=True)
-
-        over_bands(lo, hi, taps_band)
+    lane = lax.rem(lane_i + (lanes - extra), lanes)
+    tap_e = lane % rows_all
+    source_e = rows_all - 1 - row_i + tap_e - half
+    valid = (lane < ks * rows_all) & (tap_e < ks) & (source_e >= 0) & (source_e < rows_all)
+    diag_mask[...] = jnp.where(valid, 1.0, 0.0)
+
+    def taps_band(b):
+        rows_b = slope[pl.ds(b, rows_all, stride=fs), :].astype(BF16)
+        cross = mm_nt(rows_b, stack[b])
+        moved = pltpu.roll(cross, (skew + extra) % lanes, 1, stride=1, stride_axis=0)
+        moved = moved * diag_mask[...]
+        acc = moved[0:8]
+        for r in range(8, rows_all, 8):
+            acc = acc + moved[r:r + 8]
+        for part in range(lanes // 128):
+            sums[part, pl.ds(pl.multiple_of(b * 8, 8), 8), :] = acc[:, part * 128:(part + 1) * 128]
 
     for c in range(chunks):
         slope_rows(me_b * rows + c * step_rows)
-    if split:
-        taps_part(0, (1 - me_b) * rows, rows, 0, groups)
-
-    each(nd, lambda k: scatter_early(k).wait_recv())
-    early_x[0] = add_up(early, early_in, ew)
-    for k in range(1, nb):
-        band_early(k).start()
-
     for k in range(1, nb):
         source = lax.rem(me_b + nb - k, nb)
         for c in range(chunks):
             d_copy(k, c).wait_recv()
             slope_rows(source * rows + c * step_rows)
 
-    first_g[:, 0:bp] = hid_s[...]
-    each(nd, lambda k: scatter_first(k).start())
-    own = early_x[0]
+    early[:, 0:outs] = g_out
+    early[:, outs:outs + ch] = g_mid
+    early[:, outs + ch:outs + ch + bands] = hid_s[:, 0:bands]
+    scatter(early, early_in, ew, e_ss, e_rs)
+
+    first, second = groups * 2 // 5, groups * 7 // 10
+    over_bands(0, first, taps_band)
+
+    wait_all(early_in, e_rs)
+    early_out[me_d, me_b] = add_up(early, early_in, ew)
+    for k in range(1, nb):
+        band_early(k).start()
+
+    over_bands(first, second, taps_band)
+
     for k in range(1, nb):
         band_early(k).wait_recv()
-        own = own + early_x[k]
-    piece(early_out, me_d, ew)[...] = own
-    each(nd, lambda k: gather_early(k).start())
-
-    rest = (me_b * rows, rows) if split else (0, rows_all)
-    cut = groups // 2
-    taps_part(1, *rest, 0, cut)
-
-    each(nd, lambda k: scatter_first(k).wait_recv())
-    piece(first_out.at[me_b], me_d, gw)[...] = add_up(first_g, first_in, gw)
-    each(total, lambda k: gather_first(k).start())
-
-    taps_part(1, *rest, cut, groups)
-
-    def pick_taps(part, start):
-        slot = (8 * ks, lanes)
-        r = lax.broadcasted_iota(jnp.int32, slot, 0)
-        lane = lax.broadcasted_iota(jnp.int32, slot, 1)
-        lane = lax.rem(lane + start + (lanes - extra), lanes)
-        spot = jnp.where(lane == (r % 8) * rows_all + r // 8, 1.0, 0.0)
-        return lax.dot_general(
-            spot, sums[part], (((1,), (1,)), ((), ())),
-            preferred_element_type=F32, precision=lax.Precision.HIGHEST,
-        )
-
-    taps_sum = pick_taps(1, rest[0])
-    if split:
-        taps_sum = taps_sum + pick_taps(0, (1 - me_b) * rows)
-    late[0:8 * ks, 0:bp] = taps_sum
-    each(nd, lambda k: scatter_late(k).start())
-
-    each(nd, lambda k: gather_early(k).wait_recv())
-    go_ref[...] = early_out[:, 0:outs]
-    gm_ref[...] = early_out[:, outs:outs + ch]
-
-    each(nd, lambda k: scatter_late(k).wait_recv())
-    piece(gk_ref, me_d, lw)[...] = add_up(late, late_in, lw)
-    each(nd, lambda k: gather_late(k).start())
-
-    each(total, lambda k: gather_first(k).wait_recv())
+    gather(early_out, ea_ss, ea_rs)
+
+    over_bands(second, groups, taps_band)
+
+    slot_r = lax.broadcasted_iota(jnp.int32, (8 * ks, lanes), 0)
+    slot_l = lax.broadcasted_iota(jnp.int32, (8 * ks, lanes), 1) - extra
+    spot = jnp.where(slot_l == (slot_r % 8) * rows_all + slot_r // 8, 1.0, 0.0)
+    parts = []
+    for part in range(lanes // 128):
+        rows_sum = sums[part, pl.ds(0, bp, stride=8), :]
+        for r in range(1, 8):
+            rows_sum = rows_sum + sums[part, pl.ds(r, bp, stride=8), :]
+        parts.append(rows_sum)
+    per_band = wide(parts)
+    late[0:8 * ks, 0:bp] = lax.dot_general(
+        spot, per_band, (((1,), (1,)), ((), ())),
+        preferred_element_type=F32, precision=lax.Precision.HIGHEST,
+    )
+    scatter(late, late_in, lw, l_ss, l_rs)
+
+    wait_all(early_out, ea_rs)
+
+    def put_early(out, d, r, w0, w):
+        both = out[d, 0]
+        for k in range(1, nb):
+            both = both + out[d, k]
+        total_ref[r:r + 8, w0:w0 + w] = both
+        for k in range(nb):
+            sides[k, r:r + 8, w0:w0 + w] = out[d, k]
+
+    spread_out(early_out, ew, put_early)
+    go_ref[...] = total_ref[:, 0:outs]
+    gm_ref[...] = total_ref[:, outs:outs + ch]
     for k in range(nb):
-        gf_ref[:, k * bands:(k + 1) * bands] = first_out[k, :, 0:bands]
-    each(nd, lambda k: gather_late(k).wait_recv())
-
+        gf_ref[:, k * bands:(k + 1) * bands] = sides[k, :, outs + ch:outs + ch + bands]
+
+    wait_all(late_in, l_rs)
+    late_out[me_d] = add_up(late, late_in, lw)
+    gather(late_out, la_ss, la_rs)
     for k in range(1, nb):
         band_early(k).wait_send()
         for c in range(chunks):
             z_copy(k, c).wait_send()
             d_copy(k, c).wait_send()
-    each(nd, lambda k: scatter_early(k).wait_send())
-    each(nd, lambda k: gather_early(k).wait_send())
-    each(nd, lambda k: scatter_first(k).wait_send())
-    each(total, lambda k: gather_first(k).wait_send())
-    each(nd, lambda k: scatter_late(k).wait_send())
-    each(nd, lambda k: gather_late(k).wait_send())
+    wait_all(early_in, e_ss)
+    wait_all(early_out, ea_ss)
+    wait_all(late_in, l_ss)
+    wait_all(late_out, la_rs)
+
+    def put_late(out, d, r, w0, w):
+        gk_ref[r:r + 8, w0:w0 + w] = out[d]
+
+    spread_out(late_out, lw, put_late)
+    wait_all(late_out, la_ss)
 
 
 def finish(gk_in, gf_in, gm_in, go_in, gk_out, gf_out, gm_out, go_out):
@@ -470,12 +452,11 @@
     ts = rows + 8 if rows % 16 == 0 and outs % 8 == 0 else rows
     lane_parts = nd // 8
     lanes = 8 * rows_all
-    ew = up(outs + ch, 128 * lane_parts)
-    gw = up(bp, 128 * lane_parts)
+    ew = up(outs + ch + bands, 128 * lane_parts)
     lw = up(bp, 128 * lane_parts)
     cfg = dict(
         nd=nd, nb=nb, bands=bands, unroll=unroll, bp=bp, ks=ks, rows_all=rows_all, rows=rows,
-        width=width, chunks=chunks, ch=ch, outs=outs, ew=ew, gw=gw, lw=lw, fs=fs, ts=ts,
+        width=width, chunks=chunks, ch=ch, outs=outs, ew=ew, lw=lw, fs=fs, ts=ts,
         scale=1.0 / math.sqrt(nd * rows_all * width),
     )
     sems = lambda *shape: pltpu.SemaphoreType.DMA(shape)
@@ -491,6 +472,9 @@
         in_specs=[vmem] * 7,
         out_specs=(vmem,) * 4,
         scratch_shapes=[
+            pltpu.VMEM((rows_all, lanes), F32),
+            pltpu.VMEM((ks, rows_all, width), BF16),
+            pltpu.VMEM((rows_all, lanes), F32),
             pltpu.VMEM((bp, lanes), F32),
             pltpu.VMEM((bands, rows_all // 2, lanes), BF16),
             pltpu.VMEM((ch, bp), BF16),
@@ -498,7 +482,7 @@
             pltpu.VMEM((ch, ch), BF16),
             pltpu.VMEM((outs, ch), BF16),
             pltpu.VMEM((outs * ts, width), F32),
-            pltpu.VMEM((2, bp, lanes), F32),
+            pltpu.VMEM((lanes // 128, 8 * bp, 128), F32),
             pltpu.VMEM((bands, lanes, width), BF16),
             pltpu.VMEM((rows_all * fs, width), F32),
             pltpu.VMEM((rows_all * fs, width), F32),
@@ -508,17 +492,14 @@
             pltpu.VMEM((ch, bp), F32),
             pltpu.VMEM((64, ew), F32),
             pltpu.VMEM((nd, 8, ew // lane_parts), F32),
-            pltpu.VMEM((nb, 8, ew // lane_parts), F32),
+            pltpu.VMEM((nd, nb, 8, ew // lane_parts), F32),
             pltpu.VMEM((64, ew), F32),
-            pltpu.VMEM((64, gw), F32),
-            pltpu.VMEM((nd, 8, gw // lane_parts), F32),
-            pltpu.VMEM((nb, 64, gw), F32),
+            pltpu.VMEM((nb, 64, ew), F32),
             pltpu.VMEM((64, lw), F32),
             pltpu.VMEM((nd, 8, lw // lane_parts), F32),
+            pltpu.VMEM((nd, 8, lw // lane_parts), F32),
             sems(nb, chunks), sems(nb, chunks), sems(nb, chunks), sems(nb, chunks),
-            sems(nd), sems(nd), sems(nb), sems(nb), sems(nd), sems(nd),
-            sems(nd), sems(nd), sems(nd * nb), sems(nd * nb),
-            sems(nd), sems(nd), sems(nd), sems(nd),
+            sems(nb), sems(nb), *[pltpu.SemaphoreType.DMA] * 8,
         ],
         compiler_params=pltpu.CompilerParams(
             collective_id=0, has_side_effects=True, vmem_limit_bytes=56 * 1024 * 1024

time: 55.9 us -> 54 us (0.966)
  Pallas kernels: 55.1 us -> 53.2 us
    pallas_call x1, Pallas kernels: 53.4 us -> 51.4 us  [on_device(): pl.pallas_call(functools.partial(kernel, cfg), out_shape=(jax.ShapeDtypeS...]
where the time goes in v4:
time: 54 us; the launch traced here: 53.8 us
  Pallas kernels  53.2 us (99%)
  between operations  0.64 us (1%)
    pallas_call x1, Pallas kernels, on_device(): pl.pallas_call(functools.partial(kernel, cfg), out_shape=(jax.ShapeDtypeS...  51.4 us
    pallas_call x1, Pallas kernels, on_device(): pl.pallas_call(finish, out_shape=(jax.ShapeDtypeStruct((ks, ks, bands), F...  1.71 us

profile of v4, /device:TPU:0, one launch (start us, length us, event | category | flops | bytes accessed | tf_op | source)
XLA Modules:
  0.0 53.8 jit_solution(5263627416462248392)
XLA Ops:
  0.6 51.4 %shard_map.102 = (f32[64,256]{1,0:T(8,128)}, f32[64,280]{1,0:T(8,128)}, f32[64,64]{1,0:T(8,128)}, f32[64,280]{1,0:T(8,128)}) custom-call(bf16[140,32,128]{2,1,0:T(8,128)(2,1)} %bitcast.7, bf16[7,7,140]{2,1,0:T(8,128)(2,1)} %bitcast.10, bf16[64,280]{1,0:T(8,128)(2,1)} %bitcast.9, bf16[64,64]{1,0:T(8,128)(2,1)} %wm_ref.1, bf16[64,280]{1,0:T(8,128)(2,1)} %wo_ref.1, ...), custom_call_target="tpu_custom_call" | custom-call | tf_op jit(solution)/shard_map/pallas_call | solution.py:464
  52.1 1.7 %shard_map.103 = (f32[7,7,140]{2,1,0:T(8,128)}, f32[64,280]{1,0:T(8,128)}, f32[64,64]{1,0:T(8,128)}, f32[64,280]{1,0:T(8,128)}) custom-call(f32[64,256]{1,0:T(8,128)} %get-tuple-element.12.gk_in, f32[64,280]{1,0:T(8,128)} %get-tuple-element.13.gf_in, f32[64,64]{1,0:T(8,128)} %get-tuple-element.14.gm_in, f32[64,280]{1,0:T(8,128)} %get-tuple-element.15.go_in), custom_call_target="tpu_custom_call" | custom-call | tf_op jit(solution)/shard_map/pallas_call | solution.py:511

commit v5 on v4

--- a/solution.py
+++ b/solution.py
@@ -38,7 +38,7 @@
     cfg,
     x_ref, taps_ref, w1t_ref, wm_ref, wo_ref, target_ref, mask_ref,
     gk_ref, gf_ref, gm_ref, go_ref,
-    band_mask, edge, diag_mask, tap_rows, taps_own, wft_ref, wf_ref, wmt_ref, wot_ref, wanted, sums, stack, filt, slope, z_send, z_recv, dz_all, hid_s,
+    band_mask, edge, diag_mask, tap_rows, taps_all, wft_ref, wf_ref, wmt_ref, wot_ref, wanted, sums, stack, filt, slope, z_send, z_recv, dz_all, hid_s,
     early, early_in, early_out, total_ref, sides, late, late_in, late_out,
     z_ss, z_rs, d_ss, d_rs, ex_ss, ex_rs, e_ss, e_rs, ea_ss, ea_rs, l_ss, l_rs, la_ss, la_rs,
 ):
@@ -101,48 +101,53 @@
         base = base + mm_tn(taps_ref[i], spot)
     tap_rows[0:bands, :] = base
 
-    lower = me_b == 0
-    mid_row = rows_all // 2
-
-    def filter_band(b):
+    def over_bands(lo, hi, act):
+        def body(g, _):
+            stores = [act(g * unroll + q) for q in range(unroll)]
+            for store in stores:
+                store()
+            return 0
+
+        lax.fori_loop(lo, hi, body, 0)
+
+    half_rows = rows if split else rows_all
+
+    def shift_band(b):
         image = x_ref[b]
         parts = []
         for j in range(ks):
             s = j - half
-            if s == 0:
-                moved = image
-            else:
-                moved = pltpu.roll(image, (-s) % width, 1) * edge[j]
-            parts.append(moved)
+            parts.append(image if s == 0 else pltpu.roll(image, (-s) % width, 1) * edge[j])
         parts.append(jnp.zeros((lanes - ks * rows_all, width), BF16))
-        moved_all = jnp.concatenate(parts, axis=0)
-        stack[b] = moved_all
         spread = jnp.broadcast_to(tap_rows[pl.ds(b, 1), :], (rows_all, lanes))
         taps = pltpu.roll(spread, lanes - 8, 1, stride=1, stride_axis=0)
-        taps = taps * band_mask[...]
-        if split:
-            taps_own[b] = jnp.where(lower, taps[:mid_row], taps[mid_row:]).astype(BF16)
-            taps = jnp.where(lower, taps[mid_row:], taps[:mid_row])
-            first, count = (1 - me_b) * rows, rows
-        else:
-            first, count = 0, rows_all
-        out = mm(taps.astype(BF16), moved_all)
-        filt[pl.ds(first * fs + b, count, stride=fs), :] = out.astype(BF16).astype(F32)
-
-    def filter_own(b):
-        out = mm(taps_own[b], stack[b])
-        filt[pl.ds(me_b * rows * fs + b, rows, stride=fs), :] = out.astype(BF16).astype(F32)
-
-    def over_bands(lo, hi, act):
-        def body(g, _):
-            for q in range(unroll):
-                act(g * unroll + q)
-            return 0
-
-        lax.fori_loop(lo, hi, body, 0)
+        taps = (taps * band_mask[...]).astype(BF16)
+
+        def store():
+            for j in range(len(parts)):
+                size = parts[j].shape[0]
+                stack[b, j * rows_all:j * rows_all + size, :] = parts[j]
+            for k in range(rows_all // half_rows):
+                taps_all[k, b] = taps[k * half_rows:(k + 1) * half_rows]
+
+        return store
+
+    def filter_part(part):
+        first = part * half_rows * fs
+
+        def filter_band(b):
+            out = mm(taps_all[part, b], stack[b]).astype(BF16).astype(F32)
+
+            def store():
+                filt[pl.ds(first + b, half_rows, stride=fs), :] = out
+
+            return store
+
+        over_bands(0, groups, filter_band)
 
     groups = bands // unroll
-    over_bands(0, groups, filter_band)
+    over_bands(0, groups, shift_band)
+    filter_part(1 - me_b if split else 0)
 
     pick = jnp.where(
         lax.broadcasted_iota(jnp.int32, (bp, outs), 1)
@@ -191,7 +196,7 @@
             z_part(k, c)
             z_copy(k, c).start()
     if split:
-        over_bands(0, groups, filter_own)
+        filter_part(me_b)
     for c in range(chunks):
         z_part(0, c)
     wf_ref[...] = mm_nt(pick, w1t_ref[...]).astype(BF16)
@@ -345,8 +350,13 @@
         acc = moved[0:8]
         for r in range(8, rows_all, 8):
             acc = acc + moved[r:r + 8]
-        for part in range(lanes // 128):
-            sums[part, pl.ds(pl.multiple_of(b * 8, 8), 8), :] = acc[:, part * 128:(part + 1) * 128]
+
+        def store():
+            place = pl.ds(pl.multiple_of(b * 8, 8), 8)
+            for part in range(lanes // 128):
+                sums[part, place, :] = acc[:, part * 128:(part + 1) * 128]
+
+        return store
 
     for c in range(chunks):
         slope_rows(me_b * rows + c * step_rows)
@@ -476,7 +486,7 @@
             pltpu.VMEM((ks, rows_all, width), BF16),
             pltpu.VMEM((rows_all, lanes), F32),
             pltpu.VMEM((bp, lanes), F32),
-            pltpu.VMEM((bands, rows_all // 2, lanes), BF16),
+            pltpu.VMEM((2, bands, rows_all // 2, lanes) if nb == 2 else (1, bands, rows_all, lanes), BF16),
             pltpu.VMEM((ch, bp), BF16),
             pltpu.VMEM((bp, ch), BF16),
             pltpu.VMEM((ch, ch), BF16),

time: 54 us -> 55.2 us (1.022)
  Pallas kernels: 53.2 us -> 54.4 us
    pallas_call x1, Pallas kernels: 51.4 us -> 52.7 us  [on_device(): pl.pallas_call(functools.partial(kernel, cfg), out_shape=(jax.ShapeDtypeS...]
where the time goes in v5:
time: 55.2 us; the launch traced here: 55 us
  Pallas kernels  54.4 us (99%)
  between operations  0.64 us (1%)
    pallas_call x1, Pallas kernels, on_device(): pl.pallas_call(functools.partial(kernel, cfg), out_shape=(jax.ShapeDtypeS...  52.7 us
    pallas_call x1, Pallas kernels, on_device(): pl.pallas_call(finish, out_shape=(jax.ShapeDtypeStruct((ks, ks, bands), F...  1.71 us

profile of v5, /device:TPU:0, one launch (start us, length us, event | category | flops | bytes accessed | tf_op | source)
XLA Modules:
  0.0 55.0 jit_solution(8281247451170420599)
XLA Ops:
  0.6 52.7 %shard_map.102 = (f32[64,256]{1,0:T(8,128)}, f32[64,280]{1,0:T(8,128)}, f32[64,64]{1,0:T(8,128)}, f32[64,280]{1,0:T(8,128)}) custom-call(bf16[140,32,128]{2,1,0:T(8,128)(2,1)} %bitcast.7, bf16[7,7,140]{2,1,0:T(8,128)(2,1)} %bitcast.10, bf16[64,280]{1,0:T(8,128)(2,1)} %bitcast.9, bf16[64,64]{1,0:T(8,128)(2,1)} %wm_ref.1, bf16[64,280]{1,0:T(8,128)(2,1)} %wo_ref.1, ...), custom_call_target="tpu_custom_call" | custom-call | tf_op jit(solution)/shard_map/pallas_call | solution.py:474
  53.3 1.7 %shard_map.103 = (f32[7,7,140]{2,1,0:T(8,128)}, f32[64,280]{1,0:T(8,128)}, f32[64,64]{1,0:T(8,128)}, f32[64,280]{1,0:T(8,128)}) custom-call(f32[64,256]{1,0:T(8,128)} %get-tuple-element.12.gk_in, f32[64,280]{1,0:T(8,128)} %get-tuple-element.13.gf_in, f32[64,64]{1,0:T(8,128)} %get-tuple-element.14.gm_in, f32[64,280]{1,0:T(8,128)} %get-tuple-element.15.go_in), custom_call_target="tpu_custom_call" | custom-call | tf_op jit(solution)/shard_map/pallas_call | solution.py:521

commit v6 on v4

--- a/solution.py
+++ b/solution.py
@@ -209,6 +209,19 @@
 
         lax.fori_loop(0, outs // 8, widen, 0)
 
+    early[...] = jnp.zeros_like(early)
+    late[...] = jnp.zeros_like(late)
+    sums[...] = jnp.zeros_like(sums)
+
+    skew = lanes - (rows_all - 1) + half
+    extra = -skew % 8
+
+    lane = lax.rem(lane_i + (lanes - extra), lanes)
+    tap_e = lane % rows_all
+    source_e = rows_all - 1 - row_i + tap_e - half
+    valid = (lane < ks * rows_all) & (tap_e < ks) & (source_e >= 0) & (source_e < rows_all)
+    diag_mask[...] = jnp.where(valid, 1.0, 0.0)
+
     def d_copy(k, c):
         part = pl.ds(me_b * rows + c * step_rows, step_rows)
         return pltpu.make_async_remote_copy(
@@ -222,6 +235,26 @@
 
     def wide(pieces):
         return jnp.concatenate(pieces, axis=1)
+
+    hid_s[...] = jnp.zeros_like(hid_s)
+
+    def slope_rows(first):
+        def one(p, _):
+            h = first + 2 * p
+            dz = wide([dz_all[h], dz_all[h + 1]])
+            hid_s[...] += mm_nt(dz, filt_rows(h, 2))
+            back = mm(wf_ref[...], dz)
+            for r in range(2):
+                place = pl.multiple_of((rows_all - 1 - h - r) * fs, 8)
+                slope[pl.ds(place, bp), :] = back[:, r * width:(r + 1) * width]
+            return 0
+
+        lax.fori_loop(0, step_rows // 2, one, 0, unroll=True)
+
+    def others_slopes(c):
+        for k in range(1, nb):
+            d_copy(k, c).wait_recv()
+            slope_rows(lax.rem(me_b + nb - k, nb) * rows + c * step_rows)
 
     g_out = jnp.zeros((ch, outs), F32)
     g_mid = jnp.zeros((ch, ch), F32)
@@ -260,6 +293,10 @@
             dz_all[me_b * rows + h] = dz[:, r * width:(r + 1) * width]
         for k in range(1, nb):
             d_copy(k, c).start()
+        slope_rows(me_b * rows + c * step_rows)
+        if c > 0:
+            others_slopes(c - 1)
+    others_slopes(chunks - 1)
 
     def piece(ref, index, w):
         lane_parts = nd // 8
@@ -308,34 +345,6 @@
         each_w = w // lane_parts
         for d in range(nd):
             put(out, d, (d // lane_parts) * 8, (d % lane_parts) * each_w, each_w)
-
-    early[...] = jnp.zeros_like(early)
-    late[...] = jnp.zeros_like(late)
-    sums[...] = jnp.zeros_like(sums)
-
-    hid_s[...] = jnp.zeros_like(hid_s)
-
-    def slope_rows(first):
-        def one(p, _):
-            h = first + 2 * p
-            dz = wide([dz_all[h], dz_all[h + 1]])
-            hid_s[...] += mm_nt(dz, filt_rows(h, 2))
-            back = mm(wf_ref[...], dz)
-            for r in range(2):
-                place = pl.multiple_of((rows_all - 1 - h - r) * fs, 8)
-                slope[pl.ds(place, bp), :] = back[:, r * width:(r + 1) * width]
-            return 0
-
-        lax.fori_loop(0, step_rows // 2, one, 0, unroll=True)
-
-    skew = lanes - (rows_all - 1) + half
-    extra = -skew % 8
-
-    lane = lax.rem(lane_i + (lanes - extra), lanes)
-    tap_e = lane % rows_all
-    source_e = rows_all - 1 - row_i + tap_e - half
-    valid = (lane < ks * rows_all) & (tap_e < ks) & (source_e >= 0) & (source_e < rows_all)
-    diag_mask[...] = jnp.where(valid, 1.0, 0.0)
 
     def taps_band(b):
         rows_b = slope[pl.ds(b, rows_all, stride=fs), :].astype(BF16)
@@ -347,14 +356,6 @@
             acc = acc + moved[r:r + 8]
         for part in range(lanes // 128):
             sums[part, pl.ds(pl.multiple_of(b * 8, 8), 8), :] = acc[:, part * 128:(part + 1) * 128]
-
-    for c in range(chunks):
-        slope_rows(me_b * rows + c * step_rows)
-    for k in range(1, nb):
-        source = lax.rem(me_b + nb - k, nb)
-        for c in range(chunks):
-            d_copy(k, c).wait_recv()
-            slope_rows(source * rows + c * step_rows)
 
     early[:, 0:outs] = g_out
     early[:, outs:outs + ch] = g_mid
@@ -445,7 +446,7 @@
     ch = w_first.shape[1]
     outs = w_out.shape[1]
     rows = rows_all // nb
-    chunks = min(4, rows // 2)
+    chunks = min(8, rows // 2)
     unroll = max(u for u in range(1, 11) if bands % u == 0)
     bp = up(bands, 16)
     fs = bp + 8

time: 54 us -> 62.1 us (1.15)
  Pallas kernels: 53.2 us -> 61.3 us
    pallas_call x1, Pallas kernels: 51.4 us -> 59.6 us  [on_device(): pl.pallas_call(functools.partial(kernel, cfg), out_shape=(jax.ShapeDtypeS...]
where the time goes in v6:
time: 62.1 us; the launch traced here: 61.9 us
  Pallas kernels  61.3 us (99%)
  between operations  0.64 us (1%)
    pallas_call x1, Pallas kernels, on_device(): pl.pallas_call(functools.partial(kernel, cfg), out_shape=(jax.ShapeDtypeS...  59.6 us
    pallas_call x1, Pallas kernels, on_device(): pl.pallas_call(finish, out_shape=(jax.ShapeDtypeStruct((ks, ks, bands), F...  1.71 us

profile of v6, /device:TPU:0, one launch (start us, length us, event | category | flops | bytes accessed | tf_op | source)
XLA Modules:
  0.0 61.9 jit_solution(323045765488198695)
XLA Ops:
  0.6 59.6 %shard_map.102 = (f32[64,256]{1,0:T(8,128)}, f32[64,280]{1,0:T(8,128)}, f32[64,64]{1,0:T(8,128)}, f32[64,280]{1,0:T(8,128)}) custom-call(bf16[140,32,128]{2,1,0:T(8,128)(2,1)} %bitcast.7, bf16[7,7,140]{2,1,0:T(8,128)(2,1)} %bitcast.10, bf16[64,280]{1,0:T(8,128)(2,1)} %bitcast.9, bf16[64,64]{1,0:T(8,128)(2,1)} %wm_ref.1, bf16[64,280]{1,0:T(8,128)(2,1)} %wo_ref.1, ...), custom_call_target="tpu_custom_call" | custom-call | tf_op jit(solution)/shard_map/pallas_call | solution.py:465
  60.2 1.7 %shard_map.103 = (f32[7,7,140]{2,1,0:T(8,128)}, f32[64,280]{1,0:T(8,128)}, f32[64,64]{1,0:T(8,128)}, f32[64,280]{1,0:T(8,128)}) custom-call(f32[64,256]{1,0:T(8,128)} %get-tuple-element.12.gk_in, f32[64,280]{1,0:T(8,128)} %get-tuple-element.13.gf_in, f32[64,64]{1,0:T(8,128)} %get-tuple-element.14.gm_in, f32[64,280]{1,0:T(8,128)} %get-tuple-element.15.go_in), custom_call_target="tpu_custom_call" | custom-call | tf_op jit(solution)/shard_map/pallas_call | solution.py:512

commit v7 on v4

--- a/solution.py
+++ b/solution.py
@@ -177,14 +177,10 @@
     def z_part(k, c):
         owner = lax.rem(me_b + k, nb)
 
-        def one(p, _):
-            h = c * step_rows + p * 2
-            z = mm(wft_ref[...], filt_rows(owner * rows + h, 2))
-            z_send[k, h] = z[:, :width]
-            z_send[k, h + 1] = z[:, width:]
-            return 0
-
-        lax.fori_loop(0, step_rows // 2, one, 0, unroll=True)
+        h = c * step_rows
+        z = mm(wft_ref[...], filt_rows(owner * rows + h, step_rows))
+        for r in range(step_rows):
+            z_send[k, h + r] = z[:, r * width:(r + 1) * width]
 
     for k in range(1, nb):
         for c in range(chunks):
@@ -316,17 +312,12 @@
     hid_s[...] = jnp.zeros_like(hid_s)
 
     def slope_rows(first):
-        def one(p, _):
-            h = first + 2 * p
-            dz = wide([dz_all[h], dz_all[h + 1]])
-            hid_s[...] += mm_nt(dz, filt_rows(h, 2))
-            back = mm(wf_ref[...], dz)
-            for r in range(2):
-                place = pl.multiple_of((rows_all - 1 - h - r) * fs, 8)
-                slope[pl.ds(place, bp), :] = back[:, r * width:(r + 1) * width]
-            return 0
-
-        lax.fori_loop(0, step_rows // 2, one, 0, unroll=True)
+        dz = wide([dz_all[first + r] for r in range(step_rows)])
+        hid_s[...] += mm_nt(dz, filt_rows(first, step_rows))
+        back = mm(wf_ref[...], dz)
+        for r in range(step_rows):
+            place = pl.multiple_of((rows_all - 1 - first - r) * fs, 8)
+            slope[pl.ds(place, bp), :] = back[:, r * width:(r + 1) * width]
 
     skew = lanes - (rows_all - 1) + half
     extra = -skew % 8
@@ -445,7 +436,7 @@
     ch = w_first.shape[1]
     outs = w_out.shape[1]
     rows = rows_all // nb
-    chunks = min(4, rows // 2)
+    chunks = min(2, rows // 2)
     unroll = max(u for u in range(1, 11) if bands % u == 0)
     bp = up(bands, 16)
     fs = bp + 8

time: 54 us -> 54.5 us (level)
  no operation moved by 1% of the time
where the time goes in v7:
time: 54.5 us; the launch traced here: 54.3 us
  Pallas kernels  53.7 us (99%)
  between operations  0.64 us (1%)
    pallas_call x1, Pallas kernels, on_device(): pl.pallas_call(functools.partial(kernel, cfg), out_shape=(jax.ShapeDtypeS...  52 us
    pallas_call x1, Pallas kernels, on_device(): pl.pallas_call(finish, out_shape=(jax.ShapeDtypeStruct((ks, ks, bands), F...  1.71 us

profile of v7, /device:TPU:0, one launch (start us, length us, event | category | flops | bytes accessed | tf_op | source)
XLA Modules:
  0.0 54.3 jit_solution(2830539409767523185)
XLA Ops:
  0.6 52.0 %shard_map.102 = (f32[64,256]{1,0:T(8,128)}, f32[64,280]{1,0:T(8,128)}, f32[64,64]{1,0:T(8,128)}, f32[64,280]{1,0:T(8,128)}) custom-call(bf16[140,32,128]{2,1,0:T(8,128)(2,1)} %bitcast.7, bf16[7,7,140]{2,1,0:T(8,128)(2,1)} %bitcast.10, bf16[64,280]{1,0:T(8,128)(2,1)} %bitcast.9, bf16[64,64]{1,0:T(8,128)(2,1)} %wm_ref.1, bf16[64,280]{1,0:T(8,128)(2,1)} %wo_ref.1, ...), custom_call_target="tpu_custom_call" | custom-call | tf_op jit(solution)/shard_map/pallas_call | solution.py:455
  52.6 1.7 %shard_map.103 = (f32[7,7,140]{2,1,0:T(8,128)}, f32[64,280]{1,0:T(8,128)}, f32[64,64]{1,0:T(8,128)}, f32[64,280]{1,0:T(8,128)}) custom-call(f32[64,256]{1,0:T(8,128)} %get-tuple-element.12.gk_in, f32[64,280]{1,0:T(8,128)} %get-tuple-element.13.gf_in, f32[64,64]{1,0:T(8,128)} %get-tuple-element.14.gm_in, f32[64,280]{1,0:T(8,128)} %get-tuple-element.15.go_in), custom_call_target="tpu_custom_call" | custom-call | tf_op jit(solution)/shard_map/pallas_call | solution.py:502

commit v8 on v7

--- a/solution.py
+++ b/solution.py
@@ -436,7 +436,7 @@
     ch = w_first.shape[1]
     outs = w_out.shape[1]
     rows = rows_all // nb
-    chunks = min(2, rows // 2)
+    chunks = min(4, rows // 2)
     unroll = max(u for u in range(1, 11) if bands % u == 0)
     bp = up(bands, 16)
     fs = bp + 8

time: 54.5 us -> 54 us (level)
  no operation moved by 1% of the time
where the time goes in v8:
time: 54 us; the launch traced here: 53.8 us
  Pallas kernels  53.2 us (99%)
  between operations  0.64 us (1%)
    pallas_call x1, Pallas kernels, on_device(): pl.pallas_call(functools.partial(kernel, cfg), out_shape=(jax.ShapeDtypeS...  51.5 us
    pallas_call x1, Pallas kernels, on_device(): pl.pallas_call(finish, out_shape=(jax.ShapeDtypeStruct((ks, ks, bands), F...  1.71 us

profile of v8, /device:TPU:0, one launch (start us, length us, event | category | flops | bytes accessed | tf_op | source)
XLA Modules:
  0.0 53.8 jit_solution(17084735145304110716)
XLA Ops:
  0.6 51.5 %shard_map.102 = (f32[64,256]{1,0:T(8,128)}, f32[64,280]{1,0:T(8,128)}, f32[64,64]{1,0:T(8,128)}, f32[64,280]{1,0:T(8,128)}) custom-call(bf16[140,32,128]{2,1,0:T(8,128)(2,1)} %bitcast.7, bf16[7,7,140]{2,1,0:T(8,128)(2,1)} %bitcast.10, bf16[64,280]{1,0:T(8,128)(2,1)} %bitcast.9, bf16[64,64]{1,0:T(8,128)(2,1)} %wm_ref.1, bf16[64,280]{1,0:T(8,128)(2,1)} %wo_ref.1, ...), custom_call_target="tpu_custom_call" | custom-call | tf_op jit(solution)/shard_map/pallas_call | solution.py:455
  52.1 1.7 %shard_map.103 = (f32[7,7,140]{2,1,0:T(8,128)}, f32[64,280]{1,0:T(8,128)}, f32[64,64]{1,0:T(8,128)}, f32[64,280]{1,0:T(8,128)}) custom-call(f32[64,256]{1,0:T(8,128)} %get-tuple-element.12.gk_in, f32[64,280]{1,0:T(8,128)} %get-tuple-element.13.gf_in, f32[64,64]{1,0:T(8,128)} %get-tuple-element.14.gm_in, f32[64,280]{1,0:T(8,128)} %get-tuple-element.15.go_in), custom_call_target="tpu_custom_call" | custom-call | tf_op jit(solution)/shard_map/pallas_call | solution.py:502
